TPU v7x, 32 devices: a whole 2x2x4 slice. The times are simulated.
32 devices in a mesh: dp: 8 (over y, x, core), mp: 4 (over z).
Axes of the slice: x: 2, y: 2, z: 4, core: 2. Of those that a mesh axis runs over, the one named last changes fastest.
Arguments:
- tokens: bfloat16 [16384, 768], P('dp'), may hold values from -6 to 6
- seg_ids: int32 [16384], P('dp'), may hold values from 0 to 64, as said below
- qkv_weight: bfloat16 [3, 768, 768], P(None, None, 'mp'), may hold values from -0.21875 to 0.21875
- qkv_bias: float32 [3, 768], P(None, 'mp'), may hold values from -3 to 3
- out_weight: bfloat16 [768, 768], P('mp'), may hold values from -0.875 to 0.875
- out_bias: float32 [768], replicated, may hold values from -2 to 2
- up_weight: bfloat16 [768, 3072], P(None, 'mp'), may hold values from -0.21875 to 0.21875
- up_bias: float32 [3072], P('mp'), may hold values from -3 to 3
- down_weight: bfloat16 [3072, 768], P('mp'), may hold values from -0.109375 to 0.109375
- down_bias: float32 [768], replicated, may hold values from -2 to 2
- norm1_gain: float32 [768], replicated, may hold values from 0.5 to 1.5
- norm1_shift: float32 [768], replicated, may hold values from -2 to 2
- query_gain: float32 [64], replicated, may hold values from 0.5 to 1.5
- query_shift: float32 [64], replicated, may hold values from -2 to 2
- key_gain: float32 [64], replicated, may hold values from 0.5 to 1.5
- norm2_gain: float32 [768], replicated, may hold values from 0.5 to 1.5
- norm2_shift: float32 [768], replicated, may hold values from -2 to 2
- cotangent: bfloat16 [16384, 768], P('dp'), may hold values from -6 to 6
Outputs:
- block_out: bfloat16 [16384, 768], P(('dp', 'mp'))
- input_grad: bfloat16 [16384, 768], P(('dp', 'mp'))
- qkv_weight_grad: float32 [3, 768, 768], P(None, None, 'mp')
- qkv_bias_grad: float32 [3, 768], P(None, 'mp')
- out_weight_grad: float32 [768, 768], P('mp')
- out_bias_grad: float32 [768], replicated
- up_weight_grad: float32 [768, 3072], P(None, 'mp')
- up_bias_grad: float32 [3072], P('mp')
- down_weight_grad: float32 [3072, 768], P('mp')
- down_bias_grad: float32 [768], replicated
- norm1_gain_grad: float32 [768], replicated
- norm1_shift_grad: float32 [768], replicated
- query_gain_grad: float32 [64], replicated
- query_shift_grad: float32 [64], replicated
- key_gain_grad: float32 [64], replicated
- norm2_gain_grad: float32 [768], replicated
- norm2_shift_grad: float32 [768], replicated
Inputs may be any that keep to these rules, and one draw needn't show every extreme that they name: `seg_ids`: within each packed sequence of 1024 slots the ids run 1, 2, 3 and so on over whole images that are square patch grids of 16 or more patches laid end to end, followed by zeros for padding up to the sequence's end.
All inputs are finite; a program needn't handle non-finite values.
Results may differ from a plain program's by a relative error of at most 0.012.
Values sent between devices are 32-bit elements; how exact they have to be, the bound alone decides.
No kernel may reach another device: no remote copies, remote signals or barrier semaphores. Data moves between devices by JAX's collectives and lax.ppermute only.
A program may use at most 192 MiB of HBM per device.

v0:
```python
import jax
import jax.numpy as jnp
from jax import lax
from jax.sharding import PartitionSpec as P

DH = 64
SEQ_LEN = 1024


norm_eps = 1e-06


def layer_norm(values, scale_vec, offset_vec):
    average = jnp.mean(values, axis=-1, keepdims=True)
    centered = values - average
    variance = jnp.mean(centered * centered, axis=-1, keepdims=True)
    return centered * lax.rsqrt(variance + norm_eps) * scale_vec + offset_vec


def exact_gelu(values):
    return jax.nn.gelu(values, approximate=False)


def shards(
    tokens,
    seg_ids,
    qkv_weight,
    qkv_bias,
    out_weight,
    out_bias,
    up_weight,
    up_bias,
    down_weight,
    down_bias,
    norm1_gain,
    norm1_shift,
    query_gain,
    query_shift,
    key_gain,
    norm2_gain,
    norm2_shift,
    cotangent,
):
    row_count = tokens.shape[0]
    seq_count = row_count // SEQ_LEN
    local_heads = qkv_weight.shape[2] // DH
    score_scale = DH ** (-0.5)
    inputs = tokens.astype(jnp.float32)
    normed_low = layer_norm(inputs, norm1_gain, norm1_shift).astype(jnp.bfloat16)
    project = (
        jnp.einsum("td,sde->ste", normed_low, qkv_weight, preferred_element_type=jnp.float32)
        + qkv_bias[:, None, :]
    )
    head_view = project.reshape(3, seq_count, SEQ_LEN, local_heads, DH)
    query_pre = head_view[0]
    key_pre = head_view[1]
    queries = layer_norm(query_pre, query_gain, query_shift).astype(jnp.bfloat16)
    key_vectors = layer_norm(key_pre, key_gain, 0.0).astype(jnp.bfloat16)
    value_vectors = head_view[2].astype(jnp.bfloat16)
    seg_view = seg_ids.reshape(seq_count, SEQ_LEN)

    def masked_scores(queries_one, keys_one, segs_one):
        scores = (
            jnp.einsum("qhd,khd->hqk", queries_one, keys_one, preferred_element_type=jnp.float32)
            * score_scale
        )
        same_segment = segs_one[:, None] == segs_one[None, :]
        return jnp.where(same_segment[None], scores, -1e30)

    def attend_one(inputs_one):
        queries_one, keys_one, values_one, segs_one = inputs_one
        scores = masked_scores(queries_one, keys_one, segs_one)
        row_max = jnp.max(scores, axis=-1, keepdims=True)
        exponent = jnp.exp(scores - row_max)
        row_total = jnp.sum(exponent, axis=-1, keepdims=True)
        weights_low = (exponent / row_total).astype(jnp.bfloat16)
        mixture_one = jnp.einsum(
            "hqk,khd->qhd", weights_low, values_one, preferred_element_type=jnp.float32
        )
        return (mixture_one.astype(jnp.bfloat16), (row_max + jnp.log(row_total))[..., 0])

    mixture, log_total = lax.map(attend_one, (queries, key_vectors, value_vectors, seg_view))
    mixture_rows = mixture.reshape(row_count, local_heads * DH)
    attended = (
        lax.psum(jnp.dot(mixture_rows, out_weight, preferred_element_type=jnp.float32), "mp")
        + out_bias
    )
    middle = inputs + attended
    second_low = layer_norm(middle, norm2_gain, norm2_shift).astype(jnp.bfloat16)
    hidden_pre = jnp.dot(second_low, up_weight, preferred_element_type=jnp.float32) + up_bias
    hidden_low = exact_gelu(hidden_pre).astype(jnp.bfloat16)
    row_share = row_count // lax.axis_size("mp")
    first_row = lax.axis_index("mp") * row_share
    down_part = lax.psum_scatter(
        jnp.dot(hidden_low, down_weight, preferred_element_type=jnp.float32),
        "mp",
        scatter_dimension=0,
        tiled=True,
    )
    block_out = (
        lax.dynamic_slice_in_dim(middle, first_row, row_share, 0) + down_part + down_bias
    ).astype(jnp.bfloat16)
    grad_hidden = jnp.dot(cotangent, down_weight.T, preferred_element_type=jnp.float32)
    down_weight_grad = jnp.dot(hidden_low.T, cotangent, preferred_element_type=jnp.float32)
    down_bias_grad = jnp.sum(cotangent.astype(jnp.float32), axis=0)
    grad_pre = jax.vjp(exact_gelu, hidden_pre)[1](grad_hidden)[0].astype(jnp.bfloat16)
    up_weight_grad = jnp.dot(second_low.T, grad_pre, preferred_element_type=jnp.float32)
    up_bias_grad = jnp.sum(grad_pre.astype(jnp.float32), axis=0)
    grad_second = jnp.dot(grad_pre, up_weight.T, preferred_element_type=jnp.float32)
    norm2_pull = jax.vjp(layer_norm, middle, norm2_gain, norm2_shift)[1]
    grad_mid_part, norm2_gain_grad, norm2_shift_grad = norm2_pull(grad_second)
    grad_middle = cotangent.astype(jnp.float32) + lax.psum(grad_mid_part, "mp")
    grad_middle_low = grad_middle.astype(jnp.bfloat16)
    out_weight_grad = jnp.dot(mixture_rows.T, grad_middle_low, preferred_element_type=jnp.float32)
    out_bias_grad = jnp.sum(grad_middle_low.astype(jnp.float32), axis=0)
    grad_mixture = jnp.dot(
        grad_middle_low, out_weight.T, preferred_element_type=jnp.float32
    ).astype(jnp.bfloat16)
    grad_mixture = grad_mixture.reshape(seq_count, SEQ_LEN, local_heads, DH)

    def attend_back(inputs_one):
        queries_one, keys_one, values_one, segs_one, lse_one, grad_one = inputs_one
        scores = masked_scores(queries_one, keys_one, segs_one)
        attn_weights = jnp.exp(scores - lse_one[:, :, None])
        weights_low = attn_weights.astype(jnp.bfloat16)
        grad_values = jnp.einsum(
            "hqk,qhd->khd", weights_low, grad_one, preferred_element_type=jnp.float32
        )
        grad_weights = jnp.einsum(
            "qhd,khd->hqk", grad_one, values_one, preferred_element_type=jnp.float32
        )
        inner_sum = jnp.sum(grad_weights * attn_weights, axis=-1, keepdims=True)
        grad_scores = (attn_weights * (grad_weights - inner_sum)).astype(jnp.bfloat16)
        grad_queries = (
            jnp.einsum("hqk,khd->qhd", grad_scores, keys_one, preferred_element_type=jnp.float32)
            * score_scale
        )
        grad_keys = (
            jnp.einsum("hqk,qhd->khd", grad_scores, queries_one, preferred_element_type=jnp.float32)
            * score_scale
        )
        return (grad_queries, grad_keys, grad_values)

    grad_queries, grad_keys, grad_values = lax.map(
        attend_back, (queries, key_vectors, value_vectors, seg_view, log_total, grad_mixture)
    )
    query_pull = jax.vjp(layer_norm, query_pre, query_gain, query_shift)[1]
    grad_query_pre, query_gain_grad, query_shift_grad = query_pull(grad_queries)
    key_pull = jax.vjp(
        lambda key_input, gain_input: layer_norm(key_input, gain_input, 0.0), key_pre, key_gain
    )[1]
    grad_key_pre, key_gain_grad = key_pull(grad_keys)
    grad_project = (
        jnp.stack([grad_query_pre, grad_key_pre, grad_values])
        .reshape(3, row_count, local_heads * DH)
        .astype(jnp.bfloat16)
    )
    qkv_weight_grad = jnp.einsum(
        "td,ste->sde", normed_low, grad_project, preferred_element_type=jnp.float32
    )
    qkv_bias_grad = jnp.sum(grad_project.astype(jnp.float32), axis=1)
    grad_normed = jnp.einsum(
        "ste,sde->td", grad_project, qkv_weight, preferred_element_type=jnp.float32
    )
    norm1_pull = jax.vjp(layer_norm, inputs, norm1_gain, norm1_shift)[1]
    grad_input_part, norm1_gain_grad, norm1_shift_grad = norm1_pull(grad_normed)
    input_share = lax.psum_scatter(grad_input_part, "mp", scatter_dimension=0, tiled=True)
    input_grad = (
        lax.dynamic_slice_in_dim(grad_middle, first_row, row_share, 0) + input_share
    ).astype(jnp.bfloat16)
    (
        qkv_weight_grad,
        qkv_bias_grad,
        out_weight_grad,
        out_bias_grad,
        up_weight_grad,
        up_bias_grad,
        down_weight_grad,
        down_bias_grad,
    ) = lax.psum(
        (
            qkv_weight_grad,
            qkv_bias_grad,
            out_weight_grad,
            out_bias_grad,
            up_weight_grad,
            up_bias_grad,
            down_weight_grad,
            down_bias_grad,
        ),
        "dp",
    )
    (
        norm1_gain_grad,
        norm1_shift_grad,
        query_gain_grad,
        query_shift_grad,
        key_gain_grad,
        norm2_gain_grad,
        norm2_shift_grad,
    ) = lax.psum(
        (
            norm1_gain_grad,
            norm1_shift_grad,
            query_gain_grad,
            query_shift_grad,
            key_gain_grad,
            norm2_gain_grad,
            norm2_shift_grad,
        ),
        ("dp", "mp"),
    )
    return (
        block_out,
        input_grad,
        qkv_weight_grad,
        qkv_bias_grad,
        out_weight_grad,
        out_bias_grad,
        up_weight_grad,
        up_bias_grad,
        down_weight_grad,
        down_bias_grad,
        norm1_gain_grad,
        norm1_shift_grad,
        query_gain_grad,
        query_shift_grad,
        key_gain_grad,
        norm2_gain_grad,
        norm2_shift_grad,
    )


def solution(mesh):
    in_specs = (
        P("dp", None),
        P("dp"),
        P(None, None, "mp"),
        P(None, "mp"),
        P("mp", None),
        P(),
        P(None, "mp"),
        P("mp"),
        P("mp", None),
        P(),
        P(),
        P(),
        P(),
        P(),
        P(),
        P(),
        P(),
        P("dp", None),
    )
    out_specs = (
        P(("dp", "mp"), None),
        P(("dp", "mp"), None),
        P(None, None, "mp"),
        P(None, "mp"),
        P("mp", None),
        P(),
        P(None, "mp"),
        P("mp"),
        P("mp", None),
        P(),
        P(),
        P(),
        P(),
        P(),
        P(),
        P(),
        P(),
    )
    return jax.shard_map(shards, mesh=mesh, in_specs=in_specs, out_specs=out_specs, check_vma=False)
```

profile of v0, /device:TPU:0, one launch (start us, length us, event | category | flops | bytes accessed | tf_op | source)
XLA Modules:
  0.0 936.2 jit_solution(17939808307175889838)
XLA Ops:
  33.9 47.0 %while.26 = (s32[]{:T(128)}, bf16[2,1024,3,64]{1,3,2,0:T(8,128)(2,1)}, f32[2,3,1024]{2,1,0:T(4,128)}, bf16[2,1024,3,64]{1,3,2,0:T(8,128)(2,1)}, s32[2,1024]{1,0:...) while((s32[]{:T(128)}, ...), condition=%wide.region_9.10_spmd, body=%wide.region_6.9_spmd.sunk | while | flops 844297216 | bytes 53283056 | solution.py:82
  34.7 6.9 fusion.142
  41.6 7.4 fusion.143
  49.1 6.8 fusion.144
  58.1 6.9 fusion.142
  65.0 7.4 fusion.143
  72.5 6.8 fusion.144
  83.9 4.7 fusion.98
  88.6 225.7 %all-reduce.7.cloned.1.call-done = f32[2048,768]{1,0:T(8,128)} async-done(((f32[2048,768]{1,0:T(8,128)}), f32[2048,768]{1,0:T(8,128)}) %all-reduce.7.cloned.1.call-update) | async-done | bytes 6291472 | tf_op jit(solution)/shard_map/psum | solution.py:85
  314.3 4.6 fusion.96
  325.0 19.1 %convert_reduce_fusion.2 = (f32[768]{0:T(1024)}, bf16[2048,768]{1,0:T(8,128)(2,1)S(1)}, f32[2048,768]{1,0:T(8,128)}) fusion(f32[2048,768]{1,0:T(8,128)S(1)} %fusion.99, f32[768]{0:T(1024)S(1)} %copy-done.68, bf16[2048,768]{1,0:T(8,128)(2,1)S(1)} %copy-done.24, bf16[768,768]{1,0:T(8,128)(2,1)S(1)} %copy-done), kind=kOutput, calls=%fused_computation.86 | convolution fusion | flops 2533883136 | bytes 20060160 | tf_op jit(solution)/shard_map/dot_general | solution.py:103
  344.0 4.5 multiply_reduce_fusion.1
  354.7 5.7 multiply_convert_fusion.1
  362.1 4.5 fusion.100
  366.8 209.8 %all-reduce.9.cloned.1.call-done = f32[2048,768]{1,0:T(8,128)} async-done(((f32[2048,768]{1,0:T(8,128)}), f32[2048,768]{1,0:T(8,128)}) %all-reduce.9.cloned.1.call-update) | async-done | bytes 6291472 | tf_op jit(solution)/shard_map/psum | solution.py:112
  576.6 5.4 convert_reduce_fusion.3
  590.3 50.6 %while.27 = (s32[]{:T(128)}, f32[2,1024,3,64]{1,3,2,0:T(8,128)}, f32[2,1024,3,64]{1,3,2,0:T(8,128)}, bf16[2,1024,3,64]{1,3,2,0:T(8,128)(2,1)}, bf16[2,1024,3,64]...) while((s32[]{:T(128)}, f32[2,1024,3,64]{1,3,2,0:T(8,128)}, ...), condition=%wide.region_19.20_spmd, body=%wide.region_17.19_spmd.sunk | while | flops 2061890560 | bytes 138392912 | solution.py:144
  592.9 3.7 fusion.156
  596.7 7.2 multiply_reduce_fusion.11
  603.8 7.1 multiply_convert_fusion.4
  618.0 3.7 fusion.156
  621.8 7.2 multiply_reduce_fusion.11
  629.0 7.1 multiply_convert_fusion.4
  660.9 5.8 bitcast_reduce_fusion
  669.7 4.1 broadcast_add_fusion
  673.9 7.1 fusion.101
  681.0 4.2 fusion.102
  687.3 3.6 fusion.73
  691.5 43.8 %all-reduce = (f32[768]{0:T(1024)}, f32[768]{0:T(1024)}, f32[64]{0:T(128)}, f32[64]{0:T(128)}, f32[64]{0:T(128)}, /*index=5*/f32[768]{0:T(1024)}, f32[768]{0:T(1024)}) all-reduce(f32[768]{0:T(1024)S(1)} %get-tuple-element.184, f32[768]{0:T(1024)S(1)} %get-tuple-element.187, ...), channel_id=1, replica_groups=mesh['dp'=8,'mp'=4] {'dp','mp'}, use_global_device_ids=true, to_apply=%region_40.41 | all-reduce | flops 3264 | bytes 26112 | tf_op jit(solution)/shard_map/psum | solution.py:201
  735.7 25.3 %all-reduce.1 = (f32[3,192]{1,0:T(4,128)}, f32[768]{0:T(1024)}, f32[768]{0:T(1024)}, f32[768]{0:T(1024)}) all-reduce(f32[3,192]{1,0:T(4,128)S(1)} %convert_reduce_fusion.4, f32[768]{0:T(1024)S(1)} %copy-done.58, f32[768]{0:T(1024)S(1)} %copy-done.70, f32[768]{0:T(1024)S(1)} %copy-done.59), channel_id=1, replica_groups=mesh['dp'=8,'mp'=4] {'dp'}, use_global_device_ids=true, to_apply=%region_29.30 | all-reduce | flops 2880 | bytes 23040 | tf_op jit(solution)/shard_map/psum | solution.py:180
  763.9 39.2 %reduce-scatter.5.cloned.1.call-done = f32[512,768]{1,0:T(8,128)} async-done(((f32[2048,768]{1,0:T(8,128)}), f32[512,768]{1,0:T(8,128)}) %reduce-scatter.5.cloned.1.call-update) | async-done | bytes 1572880 | tf_op jit(solution)/shard_map/reduce_scatter | solution.py:167
  806.0 115.8 %all-reduce.11.cloned.1.call-done = (f32[3,768,192]{1,2,0:T(8,128)}, f32[192,768]{1,0:T(8,128)}, f32[768,768]{1,0:T(8,128)}, f32[768,768]{1,0:T(8,128)}) async-done(((f32[3,768,192]{1,2,0:T(8,128)}, f32[192,768]{1,0:T(8,128)}, f32[768,768]{1,0:T(8,128)}, f32[768,768]{1,0:T(8,128)}), (f32[3,768,192]{1,2,0:T(8,128)}, f32[192,768]{1,0:T(8,128)}, f32[768,768]{1,0:T(8,128)}, ...) | async-done | bytes 7077904 | tf_op jit(solution)/shard_map/psum | solution.py:180
  (293 shorter events, 109.2 us)
Async XLA Ops:
  7.2 317.4 %copy-start = (bf16[768,768]{1,0:T(8,128)(2,1)S(1)}, bf16[768,768]{1,0:T(8,128)(2,1)}, u32[]{:S(2)}) copy-start(bf16[768,768]{1,0:T(8,128)(2,1)} %param.30) | copy-start | bytes 3538948
  7.2 307.0 %all-reduce.7.cloned.1.call-start = ((), (), s32[]{:S(2)}) async-start(), calls=%async_computation.2 | async-start | bytes 12582912 | tf_op jit(solution)/shard_map/psum | solution.py:85
  20.3 9.6 %copy-start.64 = (f32[64]{0:T(128)S(1)}, f32[64]{0:T(128)}, u32[]{:S(2)}) copy-start(f32[64]{0:T(128)} %param.36) | copy-start | bytes 772
  23.9 7.9 copy-start.61
  41.6 7.4 copy-start.18
  41.6 7.4 copy-start.36
  65.0 7.4 copy-start.18
  65.0 7.4 copy-start.36
  83.9 230.4 %copy-start.73 = (f32[768]{0:T(1024)S(1)}, f32[768]{0:T(1024)}, u32[]{:S(2)}) copy-start(f32[768]{0:T(1024)} %param.27) | copy-start | bytes 9220
  88.5 488.0 %all-reduce.9.cloned.1.call-start = ((), (), s32[]{:S(2)}) async-start(), calls=%async_computation.4 | async-start | bytes 12582912 | tf_op jit(solution)/shard_map/psum | solution.py:112
  318.9 29.7 %copy-start.2 = (f32[2048,768]{1,0:T(8,128)}, f32[2048,768]{1,0:T(8,128)S(1)}, u32[]{:S(2)}) copy-start(f32[2048,768]{1,0:T(8,128)S(1)} %get-tuple-element.252) | copy-start | bytes 18874372
  325.0 19.1 %copy-start.23 = (f32[2048,768]{1,0:T(8,128)}, f32[2048,768]{1,0:T(8,128)S(1)}, u32[]{:S(2)}) copy-start(f32[2048,768]{1,0:T(8,128)S(1)} %fusion.99) | copy-start | bytes 18874372
  354.6 406.3 %reduce-scatter.3.cloned.1.call-start = ((), (), s32[]{:S(2)}) async-start(), calls=%async_computation.3 | async-start | bytes 7864320 | tf_op jit(solution)/shard_map/reduce_scatter | solution.py:94
  366.6 218.8 %copy-start.35 = (bf16[192,768]{1,0:T(8,128)(2,1)S(1)}, bf16[192,768]{1,0:T(8,128)(2,1)}, u32[]{:S(2)}) copy-start(bf16[192,768]{1,0:T(8,128)(2,1)} %param.26) | copy-start | bytes 884740
  366.6 436.5 %reduce-scatter.5.cloned.1.call-start = ((), (), s32[]{:S(2)}) async-start(), calls=%async_computation.5 | async-start | bytes 7864320 | tf_op jit(solution)/shard_map/reduce_scatter | solution.py:167
  582.0 8.3 copy-start.11
  582.0 8.3 copy-start.19
  582.0 8.3 copy-start.49
  590.3 54.2 %copy-start.32 = (f32[2,1024,3]{1,2,0:T(4,128)S(1)}, f32[2,1024,3]{1,2,0:T(4,128)}, u32[]{:S(2)}) copy-start(f32[2,1024,3]{1,2,0:T(4,128)} %copy-done.31) | copy-start | bytes 73732
  590.3 54.2 %copy-start.65 = (f32[64]{0:T(128)S(1)}, f32[64]{0:T(128)}, u32[]{:S(2)}) copy-start(f32[64]{0:T(128)} %param.36) | copy-start | bytes 772
  596.6 7.2 copy-start.39
  621.8 7.2 copy-start.39
  640.9 8.6 copy-start.46
  641.0 8.7 copy-start.40
  641.0 8.7 copy-start.42
  673.9 247.9 %all-reduce.11.cloned.1.call-start = ((), (), s32[]{:S(2)}) async-start(), calls=%async_computation.6 | async-start | bytes 14155776 | tf_op jit(solution)/shard_map/psum | solution.py:180
  673.9 11.3 %slice-start = ((s8[6291456]{0:T(1024)(128)(4,1)}), s8[4194304]{0:T(1024)(128)(4,1)S(1)}, s32[]{:S(2)}) async-start(s8[6291456]{0:T(1024)(128)(4,1)} %bitcast.171), calls=%async_computation.7 | async-start | bytes 8388608
  690.8 44.8 %copy-start.58 = (f32[768]{0:T(1024)S(1)}, f32[768]{0:T(1024)}, u32[]{:S(2)}) copy-start(f32[768]{0:T(1024)} %get-tuple-element.247) | copy-start | bytes 9220
  690.8 44.8 %copy-start.59 = (f32[768]{0:T(1024)S(1)}, f32[768]{0:T(1024)}, u32[]{:S(2)}) copy-start(f32[768]{0:T(1024)} %get-tuple-element.259) | copy-start | bytes 9220
  690.8 44.9 %copy-start.70 = (f32[768]{0:T(1024)S(1)}, f32[768]{0:T(1024)}, u32[]{:S(2)}) copy-start(f32[768]{0:T(1024)} %get-tuple-element.244) | copy-start | bytes 9220
  690.9 70.1 %copy-start.69 = (f32[768]{0:T(1024)S(1)}, f32[768]{0:T(1024)}, u32[]{:S(2)}) copy-start(f32[768]{0:T(1024)} %param.31) | copy-start | bytes 9220
  921.8 7.7 copy-start.1
  (66 other events, 237.6 us)
Sparse Core Ops, SparseCore 0:
  88.7 225.5 all-reduce.6
  354.7 221.7 all-reduce.8
  578.9 109.7 reduce-scatter.2
  690.8 112.2 reduce-scatter.4
  807.8 113.9 all-reduce.10
where the time goes:
time: 945 us; the launch traced here: 936 us
  waiting for transfers between devices  590 us (62%)
  matrix products  121 us (13%)
  other arithmetic  91 us (10%)
  blocking collectives  69 us (7%)
  local copies, waits for them, and re-layouts  48.7 us (5%)
  between operations  15 us (2%)
    psum x1, waiting for transfers between devices, shards(): lax.psum(jnp.dot(mixture_rows, out_weight, preferred_element_type=jnp.flo...  226 us
    psum x1, waiting for transfers between devices, shards(): grad_middle = cotangent.astype(jnp.float32) + lax.psum(grad_mid_part, 'mp')  210 us
    psum x1, waiting for transfers between devices, shards(): lax.psum((qkv_weight_grad, qkv_bias_grad, out_weight_grad, out_bias_grad,...  116 us
    psum x1, blocking collectives, shards(): lax.psum((norm1_gain_grad, norm1_shift_grad, query_gain_grad, query_shift...  43.8 us
    reduce_scatter x1, waiting for transfers between devices, shards(): lax.psum_scatter(grad_input_part, 'mp', scatter_dimension=0, tiled=True)  39.2 us
    psum x1, blocking collectives, shards(): lax.psum((qkv_weight_grad, qkv_bias_grad, out_weight_grad, out_bias_grad,...  25.3 us
    dot_general x1, matrix products, shards(): jnp.dot(cotangent, down_weight.T, preferred_element_type=jnp.float32)  19.1 us
  transfers between devices with their start and end apart: 5, of which 4 were waited for; matrix products, arithmetic and copies ran while one was open for 13% of the time, Pallas kernels for 0%

commit v1 on v0

v1 whole, which is shorter than its diff:
```python
import functools
import math

import jax
import jax.numpy as jnp
from jax import lax
from jax.experimental import pallas as pl
from jax.experimental.pallas import tpu as pltpu
from jax.sharding import PartitionSpec as P

F32 = jnp.float32
BF16 = jnp.bfloat16
DH = 64
SEQ_LEN = 1024
NORM_EPS = 1e-06
PIECES = 8
SEG_COLS = 128
LOG2E = math.log2(math.e)
SCALE = DH ** (-0.5)
BITS_A = (2, 4, 1)
BITS_B = (4, 2, 1)
VMEM_LIMIT = 56 * 1024 * 1024


def mm(a, b):
    return lax.dot_general(a, b, (((1,), (0,)), ((), ())), preferred_element_type=F32)


def mm_nt(a, b):
    return lax.dot_general(a, b, (((1,), (1,)), ((), ())), preferred_element_type=F32)


def mm_tn(a, b):
    return lax.dot_general(a, b, (((0,), (0,)), ((), ())), preferred_element_type=F32)


def call(kernel, out_shape, flops=0, bytes_accessed=0, **kw):
    return pl.pallas_call(
        kernel,
        out_shape=out_shape,
        compiler_params=pltpu.CompilerParams(vmem_limit_bytes=VMEM_LIMIT),
        cost_estimate=pl.CostEstimate(
            flops=flops, bytes_accessed=bytes_accessed, transcendentals=0
        ),
        **kw,
    )


def sds(shape, dtype):
    return jax.ShapeDtypeStruct(shape, dtype)


def row_norm(x):
    mean = jnp.mean(x, axis=-1, keepdims=True)
    cen = x - mean
    rstd = lax.rsqrt(jnp.mean(cen * cen, axis=-1, keepdims=True) + NORM_EPS)
    return cen * rstd, rstd


def row_norm_back(f, n, rstd):
    mean_f = jnp.mean(f, axis=-1, keepdims=True)
    mean_fn = jnp.mean(f * n, axis=-1, keepdims=True)
    return (f - mean_f - n * mean_fn) * rstd


def col_norm(x):
    mean = jnp.mean(x, axis=0, keepdims=True)
    cen = x - mean
    rstd = lax.rsqrt(jnp.mean(cen * cen, axis=0, keepdims=True) + NORM_EPS)
    return cen * rstd, rstd


def col_norm_back(f, n, rstd):
    mean_f = jnp.mean(f, axis=0, keepdims=True)
    mean_fn = jnp.mean(f * n, axis=0, keepdims=True)
    return (f - mean_f - n * mean_fn) * rstd


def lane_fold(x):
    out = x[:, :128]
    for t in range(1, x.shape[1] // 128):
        out = out + x[:, t * 128 : (t + 1) * 128]
    return out


def norm1_kernel(blk_ref, x_ref, g_ref, s_ref, out_ref):
    n, _ = row_norm(x_ref[...].astype(F32))
    out_ref[...] = (n * g_ref[...] + s_ref[...]).astype(BF16)


def build_q_aug(q_pre, qg, qs, qaug_ref):
    n, rstd = col_norm(q_pre)
    q_low = (n * qg + qs).astype(BF16)
    scaled = q_low.astype(F32) * (SCALE * LOG2E)
    hi = scaled.astype(BF16)
    lo = (scaled - hi.astype(F32)).astype(BF16)
    qaug_ref[0:DH, :] = hi
    qaug_ref[DH : 2 * DH, :] = lo
    return n, rstd, q_low


def build_k_aug(k_pre, kg, kaug_ref):
    n, rstd = col_norm(k_pre)
    k_low = (n * kg).astype(BF16)
    kaug_ref[:, 0 : 2 * DH] = jnp.concatenate([k_low, k_low], axis=0).T
    return n, rstd, k_low


def attn_fwd_kernel(
    idx_ref, x_ref, w_ref, b_ref, qg_ref, qs_ref, kg_ref, kmask_ref, qhot_ref,
    qpre_ref, kpre_ref, vt_ref, wt_ref, mixt_ref, mix_ref, l_ref,
    qaug_ref, kaug_ref,
):
    part = 24
    e = PIECES * part
    rows = qhot_ref.shape[1]
    heads = e // DH
    for s in range(3):
        w = jnp.concatenate(
            [w_ref[idx_ref[p], s * part : (s + 1) * part, :] for p in range(PIECES)], axis=0
        ).astype(BF16)
        wt_ref[s * e : (s + 1) * e, :] = w
    qpre_ref[...] = mm_nt(wt_ref[0:e, :], x_ref[0:rows, :]) + b_ref[0:e, :]
    kpre_ref[...] = mm_nt(wt_ref[e : 2 * e, :], x_ref[...]) + b_ref[e : 2 * e, :]
    vt_ref[...] = (mm_nt(wt_ref[2 * e : 3 * e, :], x_ref[...]) + b_ref[2 * e : 3 * e, :]).astype(
        BF16
    )
    qaug_ref[2 * DH :, :] = qhot_ref[...]
    kaug_ref[:, 2 * DH :] = kmask_ref[...]
    ones = jnp.ones((16, x_ref.shape[0]), BF16)
    for h in range(heads):
        hs = slice(h * DH, (h + 1) * DH)
        build_q_aug(qpre_ref[hs, :], qg_ref[...], qs_ref[...], qaug_ref)
        build_k_aug(kpre_ref[hs, :], kg_ref[...], kaug_ref)
        prob = jnp.exp2(mm(kaug_ref[...], qaug_ref[...])).astype(BF16)
        vaug = jnp.concatenate([vt_ref[hs, :], ones], axis=0)
        o = mm(vaug, prob)
        total = o[DH : DH + 1, :]
        l_ref[h : h + 1, :] = total
        mixt_ref[hs, :] = (o[0:DH, :] / total).astype(BF16)
    mix_ref[...] = mixt_ref[...].T


def out_norm2_kernel(
    nslot, blk_ref, *refs
):
    idxs = refs[:nslot]
    x_ref = refs[nslot]
    mixes = refs[nslot + 1 : 2 * nslot + 1]
    ws = refs[2 * nslot + 1 : 3 * nslot + 1]
    ob_ref, g_ref, s_ref = refs[3 * nslot + 1 : 3 * nslot + 4]
    mid_ref, sec_ref, ow_ref = refs[3 * nslot + 4 :]
    part = 24
    acc = x_ref[...].astype(F32) + ob_ref[...]
    for k in range(nslot):
        w = jnp.concatenate(
            [ws[k][idxs[k][p], 3 * part : 4 * part, :] for p in range(PIECES)], axis=0
        ).astype(BF16)
        ow_ref[k] = w
        acc = acc + mm(mixes[k][...], w)
    mid_ref[...] = acc
    n, _ = row_norm(acc)
    sec_ref[...] = (n * g_ref[...] + s_ref[...]).astype(BF16)


def mlp_kernel(first, *refs):
    if first:
        (sec_ref, cot_ref, ua_ref, ub_ref, ba_ref, bb_ref, da_ref, db_ref) = refs[:8]
        outs = refs[8:]
    else:
        (sec_ref, cot_ref, ua_ref, ub_ref, ba_ref, bb_ref, da_ref, db_ref, acc_in, gs_in) = refs[:10]
        outs = refs[10:]
    (acc_ref, gs_ref, gua_ref, gub_ref, gda_ref, gdb_ref, gba_ref, gbb_ref) = outs
    part = ua_ref.shape[1]
    up = jnp.concatenate([ua_ref[0], ub_ref[0]], axis=0).astype(BF16)
    down = jnp.concatenate([da_ref[0], db_ref[0]], axis=0).astype(BF16)
    bias = jnp.concatenate([ba_ref[0], bb_ref[0]], axis=1)
    sec = sec_ref[...]
    cot = cot_ref[...]
    pre = mm_nt(sec, up) + bias
    cdf = 0.5 * (1.0 + lax.erf(pre * (1.0 / math.sqrt(2.0))))
    hid = (pre * cdf).astype(BF16)
    pdf = jnp.exp(-0.5 * pre * pre) * (1.0 / math.sqrt(2.0 * math.pi))
    gpre_f = mm_nt(cot, down) * (cdf + pre * pdf)
    gpre = gpre_f.astype(BF16)
    gb = jnp.sum(gpre.astype(F32), axis=0, keepdims=True)
    gba_ref[0] = gb[:, :part]
    gbb_ref[0] = gb[:, part:]
    acc_new = mm(hid, down)
    gs_new = mm(gpre, up)
    if first:
        @pl.when(pl.program_id(0) == 0)
        def _():
            acc_ref[...] = acc_new
            gs_ref[...] = gs_new

        @pl.when(pl.program_id(0) > 0)
        def _():
            acc_ref[...] += acc_new
            gs_ref[...] += gs_new
    else:
        @pl.when(pl.program_id(0) == 0)
        def _():
            acc_ref[...] = acc_in[...] + acc_new
            gs_ref[...] = gs_in[...] + gs_new

        @pl.when(pl.program_id(0) > 0)
        def _():
            acc_ref[...] += acc_new
            gs_ref[...] += gs_new
    gd = mm_tn(hid, cot)
    gda_ref[0] = gd[:part]
    gdb_ref[0] = gd[part:]
    gu = mm_tn(gpre, sec)
    gua_ref[0] = gu[:part]
    gub_ref[0] = gu[part:]


def mid_kernel(
    nslot, idx_ref, mid_ref, acc_ref, gs_ref, cot_ref, db_ref, g_ref, ow_ref, *refs
):
    mixts = refs[:nslot]
    bo_ref, gm_ref, gmt_ref, gow_ref, st_ref = refs[nslot:]
    part = 24
    mid = mid_ref[...]
    bo_ref[...] = (mid + acc_ref[...] + db_ref[...]).astype(BF16)
    n, rstd = row_norm(mid)
    e = gs_ref[...]
    cot = cot_ref[...].astype(F32)
    gm = cot + row_norm_back(e * g_ref[...], n, rstd)
    gm_ref[...] = gm
    gm_low = gm.astype(BF16)
    st_ref[0:1, :] = jnp.sum(e * n, axis=0, keepdims=True)
    st_ref[1:2, :] = jnp.sum(e, axis=0, keepdims=True)
    st_ref[2:3, :] = jnp.sum(gm_low.astype(F32), axis=0, keepdims=True)
    st_ref[3:4, :] = jnp.sum(cot, axis=0, keepdims=True)
    st_ref[4:8, :] = jnp.zeros((4, mid.shape[1]), F32)
    for k in range(nslot):
        gmt_ref[k] = mm_nt(ow_ref[k], gm_low).astype(BF16)
        g = mm(mixts[k][...], gm_low)
        for p in range(PIECES):
            gow_ref[idx_ref[p], k * part : (k + 1) * part, :] = g[p * part : (p + 1) * part, :]


def attn_bwd_kernel(
    first, idx_ref, x_ref, qpre_ref, kpre_ref, vt_ref, wt_ref, gmt_ref, mixt_ref, l_ref,
    qg_ref, qs_ref, kg_ref, kmask_ref, qhot_ref, *refs
):
    if first:
        gw_ref, gn_ref, st_ref, gb_ref, qaug_ref, kaug_ref, gpt_ref = refs
    else:
        gn_in, gw_ref, gn_ref, st_ref, gb_ref, qaug_ref, kaug_ref, gpt_ref = refs
    part = 24
    e = PIECES * part
    rows = qhot_ref.shape[1]
    full = x_ref.shape[0]
    heads = e // DH
    qaug_ref[2 * DH :, :] = qhot_ref[...]
    kaug_ref[:, 2 * DH :] = kmask_ref[...]
    qg, qs, kg = qg_ref[...], qs_ref[...], kg_ref[...]
    qg_sum = jnp.zeros((DH, 128), F32)
    qs_sum = jnp.zeros((DH, 128), F32)
    kg_sum = jnp.zeros((DH, 128), F32)
    one_rows = (lax.broadcasted_iota(jnp.int32, (DH, full), 0) < 3).astype(F32).astype(BF16)
    row_no = lax.broadcasted_iota(jnp.int32, (DH, rows), 0)
    for h in range(heads):
        hs = slice(h * DH, (h + 1) * DH)
        qn, qr, q_low = build_q_aug(qpre_ref[hs, :], qg, qs, qaug_ref)
        kn, kr, k_low = build_k_aug(kpre_ref[hs, :], kg, kaug_ref)
        inv = 1.0 / l_ref[h : h + 1, :]
        go = gmt_ref[hs, :].astype(F32) * inv
        go_low = go.astype(BF16)
        delta = -jnp.sum(go * mixt_ref[hs, :].astype(F32), axis=0, keepdims=True)
        d0 = delta.astype(BF16).astype(F32)
        d1 = (delta - d0).astype(BF16).astype(F32)
        d2 = delta - d0 - d1
        extra = jnp.where(
            row_no == 0, d0, jnp.where(row_no == 1, d1, jnp.where(row_no == 2, d2, 0.0))
        ).astype(BF16)
        goaug = jnp.concatenate([go_low, extra], axis=0)
        vaug = jnp.concatenate([vt_ref[hs, :], one_rows], axis=0).T
        prob = jnp.exp2(mm(kaug_ref[...], qaug_ref[...]))
        ds = (prob * mm(vaug, goaug)).astype(BF16)
        gv = mm_nt(go_low, prob.astype(BF16))
        gk = mm_nt(q_low, ds) * SCALE
        gq = mm(k_low, ds) * SCALE
        qg_sum += lane_fold(gq * qn)
        qs_sum += lane_fold(gq)
        kg_sum += lane_fold(gk * kn)
        gpt_ref[h * DH : (h + 1) * DH, 0:rows] = col_norm_back(gq * qg, qn, qr).astype(BF16)
        gpt_ref[e + h * DH : e + (h + 1) * DH, :] = col_norm_back(gk * kg, kn, kr).astype(BF16)
        gpt_ref[2 * e + h * DH : 2 * e + (h + 1) * DH, :] = gv.astype(BF16)
    st_ref[0] = qg_sum
    st_ref[1] = qs_sum
    st_ref[2] = kg_sum
    gpq = gpt_ref[0:e, 0:rows]
    gpkv = gpt_ref[e : 3 * e, :]
    gb_ref[0:e, :] = lane_fold(gpq.astype(F32))
    gb_ref[e : 3 * e, :] = lane_fold(gpkv.astype(F32))
    gwq = mm(gpq, x_ref[0:rows, :])
    gwkv = mm(gpkv, x_ref[...])
    for p in range(PIECES):
        at = idx_ref[p]
        gw_ref[at, 0:part, :] = gwq[p * part : (p + 1) * part, :]
        gw_ref[at, part : 2 * part, :] = gwkv[p * part : (p + 1) * part, :]
        gw_ref[at, 2 * part : 3 * part, :] = gwkv[e + p * part : e + (p + 1) * part, :]
    gnq = mm_tn(gpq, wt_ref[0:e, :])
    gnkv = mm_tn(gpkv, wt_ref[e : 3 * e, :])
    if first:
        gn_ref[0:rows, :] = gnkv[0:rows] + gnq
        gn_ref[rows:, :] = gnkv[rows:]
    else:
        gn_ref[0:rows, :] = gn_in[0:rows, :] + gnkv[0:rows] + gnq
        gn_ref[rows:, :] = gn_in[rows:, :] + gnkv[rows:]


def norm1_stats_kernel(blk_ref, x_ref, gn_ref, out_ref):
    n, _ = row_norm(x_ref[...].astype(F32))
    e = gn_ref[...]

    @pl.when(pl.program_id(0) == 0)
    def _():
        out_ref[...] = jnp.zeros_like(out_ref)

    out_ref[0:1, :] += jnp.sum(e * n, axis=0, keepdims=True)
    out_ref[1:2, :] += jnp.sum(e, axis=0, keepdims=True)


def final_kernel(blk_ref, x_ref, gn_ref, got_ref, gm_ref, g_ref, out_ref):
    n, rstd = row_norm(x_ref[...].astype(F32))
    f = (gn_ref[...] + got_ref[...]) * g_ref[...]
    out_ref[...] = (gm_ref[...] + row_norm_back(f, n, rstd)).astype(BF16)


def unpack_kernel(idx_ref, s_ref, out_ref):
    groups = out_ref.shape[0]
    part = s_ref.shape[1] // groups
    for g in range(groups):
        whole = jnp.concatenate(
            [s_ref[idx_ref[p], g * part : (g + 1) * part, :] for p in range(PIECES)], axis=0
        )
        out_ref[g] = whole.T


def unpack_rows_kernel(idx_ref, s_ref, out_ref):
    part = s_ref.shape[1]
    for p in range(PIECES):
        out_ref[p * part : (p + 1) * part, :] = s_ref[idx_ref[p]]


def from_slot(a, k, size):
    return lax.ppermute(a, "mp", [(s, (s - k) % size) for s in range(size)])


def to_slot(a, k, size):
    return lax.ppermute(a, "mp", [(s, (s + k) % size) for s in range(size)])


def swap_plane(a, bit, size):
    return lax.ppermute(a, "dp", [(d, d ^ bit) for d in range(size)])


def gather_plane(piece, bits, size):
    state = piece[None]
    for bit in bits[:-1]:
        state = jnp.concatenate([state, swap_plane(state, bit, size)], axis=0)
    return state, swap_plane(state, bits[-1], size)


def gather_whole(piece, bits, size):
    return jnp.concatenate(gather_plane(piece, bits, size), axis=0)


def reduce_plane(keep, send, bits, size):
    cur = keep + swap_plane(send, bits[2], size)
    cur = cur[:2] + swap_plane(cur[2:], bits[1], size)
    cur = cur[:1] + swap_plane(cur[1:], bits[0], size)
    return cur[0]


def storage_of(r, bits):
    return sum(jnp.where((r & bit) != 0, 1 << t, 0) for t, bit in enumerate(bits))


def offset_of(s, bits):
    return sum(bit for t, bit in enumerate(bits) if (s >> t) & 1)


def shards(
    tokens,
    seg_ids,
    qkv_weight,
    qkv_bias,
    out_weight,
    out_bias,
    up_weight,
    up_bias,
    down_weight,
    down_bias,
    norm1_gain,
    norm1_shift,
    query_gain,
    query_shift,
    key_gain,
    norm2_gain,
    norm2_shift,
    cotangent,
):
    ndp = lax.axis_size("dp")
    nmp = lax.axis_size("mp")
    dp_no = lax.axis_index("dp")
    mp_no = lax.axis_index("mp")
    me = dp_no % PIECES
    row_count, width = tokens.shape
    share = row_count // nmp
    full = SEQ_LEN
    assert full == 2 * share
    e = qkv_weight.shape[2]
    part = e // PIECES
    units = up_weight.shape[1]
    upart = units // PIECES

    vmem = pl.BlockSpec(memory_space=pltpu.VMEM)
    smem = pl.BlockSpec(memory_space=pltpu.SMEM)

    qkv_t = jnp.swapaxes(qkv_weight, 1, 2).reshape(3, PIECES, part, width)
    out_p = out_weight.reshape(1, PIECES, part, width)
    att0 = (
        jnp.concatenate([qkv_t, out_p], axis=0)
        .transpose(1, 0, 2, 3)
        .reshape(PIECES, 4 * part, width)
        .astype(F32)
    )
    up_t = up_weight.T.reshape(PIECES, upart, width)
    down_p = down_weight.reshape(PIECES, upart, width)

    def pick(a, bits, s):
        return lax.dynamic_index_in_dim(a, me ^ offset_of(s, bits), 0, keepdims=False)

    up_half = [
        jnp.stack([pick(up_t, BITS_A, s) for s in half]) for half in (range(4), range(4, 8))
    ]
    down_half = [
        jnp.stack([pick(down_p, BITS_B, s) for s in half]) for half in (range(4), range(4, 8))
    ]
    ub = up_bias.reshape(PIECES, 1, upart)
    ub0 = jnp.stack([pick(ub, BITS_A, s) for s in range(PIECES)])

    att_piece = lax.dynamic_index_in_dim(att0, me, 0, keepdims=False)
    up_piece = up_half[0][0].astype(F32)
    down_piece = down_half[0][0].astype(F32)
    bias_pack = jnp.concatenate([qkv_bias.reshape(-1), ub0.reshape(-1)])

    att_bits = [BITS_A if k % 2 else BITS_B for k in range(nmp)]
    att = [att0]
    bias = [bias_pack]
    for k in range(1, nmp):
        bias.append(from_slot(bias_pack, k, nmp))
        att.append(gather_whole(from_slot(att_piece, k, nmp), att_bits[k], ndp))
    up = [up_half]
    down = [down_half]
    for k in range(1, nmp):
        up.append(gather_plane(from_slot(up_piece, k, nmp), BITS_A, ndp))
        down.append(gather_plane(from_slot(down_piece, k, nmp), BITS_B, ndp))

    idx_a = storage_of(jnp.arange(PIECES, dtype=jnp.int32) ^ me, BITS_A).astype(jnp.int32)
    idx_b = storage_of(jnp.arange(PIECES, dtype=jnp.int32) ^ me, BITS_B).astype(jnp.int32)
    idx_of = {BITS_A: idx_a, BITS_B: idx_b}
    idx_same = jnp.arange(PIECES, dtype=jnp.int32)
    att_idx = [idx_same] + [idx_of[att_bits[k]] for k in range(1, nmp)]

    block = 256
    per = share // block
    steps = 2 * per
    tile_no = jnp.arange(steps, dtype=jnp.int32)
    blk = jnp.where(tile_no < per, mp_no * per + tile_no, (mp_no ^ 1) * per + tile_no - per).astype(
        jnp.int32
    )
    row1 = lambda v: v.reshape(1, -1)
    const2 = lambda t, b: (0, 0)
    tok_spec = pl.BlockSpec((block, width), lambda t, b: (b[t], 0))
    run_spec = pl.BlockSpec((block, width), lambda t, b: (t, 0))
    vec_spec = pl.BlockSpec((1, width), const2)

    normed = call(
        norm1_kernel,
        sds((full, width), BF16),
        flops=full * width * 10,
        bytes_accessed=full * width * 4,
        grid_spec=pltpu.PrefetchScalarGridSpec(
            num_scalar_prefetch=1,
            grid=(steps,),
            in_specs=[tok_spec, vec_spec, vec_spec],
            out_specs=run_spec,
        ),
    )(blk, tokens, row1(norm1_gain), row1(norm1_shift))

    seg_own = lax.dynamic_slice_in_dim(seg_ids, mp_no * share, share, 0)
    seg_other = lax.dynamic_slice_in_dim(seg_ids, (mp_no ^ 1) * share, share, 0)
    seg_keys = jnp.concatenate([seg_own, seg_other])
    qhot = (
        lax.broadcasted_iota(jnp.int32, (SEG_COLS, share), 0) == seg_own[None, :]
    ).astype(BF16)
    kmask = jnp.where(
        lax.broadcasted_iota(jnp.int32, (full, SEG_COLS), 1) == seg_keys[:, None], 0.0, -1e30
    ).astype(BF16)
    col = lambda v: v.reshape(-1, 1)
    qg, qs, kg = col(query_gain), col(query_shift), col(key_gain)

    heads_state = []
    for k in range(nmp):
        heads_state.append(
            call(
                attn_fwd_kernel,
                (
                    sds((e, share), F32),
                    sds((e, full), F32),
                    sds((e, full), BF16),
                    sds((3 * e, width), BF16),
                    sds((e, share), BF16),
                    sds((share, e), BF16),
                    sds((8, share), F32),
                ),
                flops=2 * (full * width * e * 5 // 2 + full * share * e * 8),
                bytes_accessed=8_000_000,
                in_specs=[smem] + [vmem] * 8,
                out_specs=(vmem,) * 7,
                scratch_shapes=[
                    pltpu.VMEM((2 * DH + SEG_COLS, share), BF16),
                    pltpu.VMEM((full, 2 * DH + SEG_COLS), BF16),
                ],
            )(
                att_idx[k],
                normed,
                att[k],
                bias[k][: 3 * e].reshape(3 * e, 1),
                qg,
                qs,
                kg,
                kmask,
                qhot,
            )
        )

    own_spec = pl.BlockSpec((share, width), lambda t, b: (b[0] // per, 0))
    whole = lambda shape: pl.BlockSpec(shape, lambda t, b: (0,) * len(shape))
    middle, second, out_full = call(
        functools.partial(out_norm2_kernel, nmp),
        (
            sds((share, width), F32),
            sds((share, width), BF16),
            sds((nmp, e, width), BF16),
        ),
        flops=2 * share * width * e * nmp,
        bytes_accessed=16_000_000,
        grid_spec=pltpu.PrefetchScalarGridSpec(
            num_scalar_prefetch=1,
            grid=(1,),
            in_specs=[smem] * nmp
            + [own_spec]
            + [whole((share, e))] * nmp
            + [whole((PIECES, 4 * part, width))] * nmp
            + [whole((1, width))] * 3,
            out_specs=(
                whole((share, width)),
                whole((share, width)),
                whole((nmp, e, width)),
            ),
        ),
    )(
        blk,
        *att_idx,
        tokens,
        *[st[5] for st in heads_state],
        *att,
        row1(out_bias),
        row1(norm2_gain),
        row1(norm2_shift),
    )

    cot_own = lax.dynamic_slice_in_dim(cotangent, mp_no * share, share, 0)
    half = PIECES // 2
    piece_spec = pl.BlockSpec((1, upart, width), lambda t: (t, 0, 0))
    swap_spec = pl.BlockSpec((1, upart, width), lambda t: ((t % 2) * 2 + t // 2, 0, 0))
    bias_spec = pl.BlockSpec((1, 1, upart), lambda t: (t, 0, 0))
    rows_spec = pl.BlockSpec((share, width), lambda t: (0, 0))
    acc = None
    up_grads, down_grads, ub_grads = [], [], []
    for k in range(nmp):
        first = k == 0
        ubk = bias[k][3 * e :].reshape(PIECES, 1, upart)
        args = [second, cot_own, up[k][0], up[k][1], ubk[:half], ubk[half:], down[k][0], down[k][1]]
        specs = [rows_spec, rows_spec, piece_spec, piece_spec, bias_spec, bias_spec, swap_spec, swap_spec]
        alias = {}
        if not first:
            args += list(acc)
            specs += [rows_spec, rows_spec]
            alias = {8: 0, 9: 1}
        res = call(
            functools.partial(mlp_kernel, first),
            (
                sds((share, width), F32),
                sds((share, width), F32),
                *[sds((half, upart, width), F32)] * 4,
                *[sds((half, 1, upart), F32)] * 2,
            ),
            flops=2 * share * width * units * 6,
            bytes_accessed=16_000_000,
            grid=(half,),
            in_specs=specs,
            out_specs=(
                rows_spec,
                rows_spec,
                piece_spec,
                piece_spec,
                swap_spec,
                swap_spec,
                bias_spec,
                bias_spec,
            ),
            input_output_aliases=alias,
        )(*args)
        acc = res[:2]
        up_grads.append(reduce_plane(res[2], res[3], BITS_A, ndp))
        down_grads.append(reduce_plane(res[4], res[5], BITS_B, ndp))
        ub_grads.append(jnp.concatenate([res[6], res[7]], axis=0)[:, 0, :])

    block_out, grad_mid, gmt, out_grads, mid_stats = call(
        functools.partial(mid_kernel, nmp),
        (
            sds((share, width), BF16),
            sds((share, width), F32),
            sds((nmp, e, share), BF16),
            sds((PIECES, nmp * part, width), F32),
            sds((8, width), F32),
        ),
        flops=2 * share * width * e * nmp * 2,
        bytes_accessed=12_000_000,
        in_specs=[smem] + [vmem] * (7 + nmp),
        out_specs=(vmem,) * 5,
    )(
        idx_a,
        middle,
        acc[0],
        acc[1],
        cot_own,
        row1(down_bias),
        row1(norm2_gain),
        out_full,
        *[st[4] for st in heads_state],
    )

    gn = None
    qkv_grads, head_stats, qkvb_grads = [], [], []
    for k in range(nmp):
        first = k == 0
        st = heads_state[k]
        args = [
            idx_of[att_bits[k]], normed, st[0], st[1], st[2], st[3], gmt[k], st[4], st[6],
            qg, qs, kg, kmask, qhot,
        ]
        alias = {}
        if not first:
            args.append(gn)
            alias = {len(args) - 1: 1}
        gw, gn, hst, gb = call(
            functools.partial(attn_bwd_kernel, first),
            (
                sds((PIECES, 3 * part, width), F32),
                sds((full, width), F32),
                sds((3, DH, 128), F32),
                sds((3 * e, 128), F32),
            ),
            flops=2 * (full * width * e * 5 + full * share * e * 20),
            bytes_accessed=14_000_000,
            in_specs=[smem] + [vmem] * (len(args) - 1),
            out_specs=(vmem,) * 4,
            scratch_shapes=[
                pltpu.VMEM((2 * DH + SEG_COLS, share), BF16),
                pltpu.VMEM((full, 2 * DH + SEG_COLS), BF16),
                pltpu.VMEM((3 * e, full), BF16),
            ],
            input_output_aliases=alias,
        )(*args)
        qkv_grads.append(reduce_plane(gw[:half], gw[half:], att_bits[k], ndp))
        head_stats.append(hst)
        qkvb_grads.append(jnp.sum(gb, axis=1))

    got = lax.ppermute(gn[share:], "mp", [(s, s ^ 1) for s in range(nmp)])
    n1_stats = call(
        norm1_stats_kernel,
        sds((8, width), F32),
        flops=full * width * 10,
        bytes_accessed=full * width * 6,
        grid_spec=pltpu.PrefetchScalarGridSpec(
            num_scalar_prefetch=1,
            grid=(steps,),
            in_specs=[tok_spec, run_spec],
            out_specs=pl.BlockSpec((8, width), const2),
        ),
    )(blk, tokens, gn)
    input_grad = call(
        final_kernel,
        sds((share, width), BF16),
        flops=share * width * 20,
        bytes_accessed=share * width * 16,
        grid_spec=pltpu.PrefetchScalarGridSpec(
            num_scalar_prefetch=1,
            grid=(per,),
            in_specs=[tok_spec, run_spec, run_spec, run_spec, vec_spec],
            out_specs=run_spec,
        ),
    )(blk, tokens, gn, got, grad_mid, row1(norm1_gain))

    def finish(pieces, bits):
        total = pieces[0]
        for k in range(1, nmp):
            total = total + to_slot(pieces[k], k, nmp)
        bit = PIECES
        while bit < ndp:
            total = total + swap_plane(total, bit, ndp)
            bit *= 2
        return gather_whole(total, bits, ndp)

    up_state = finish(up_grads, BITS_A)
    down_state = finish(down_grads, BITS_B)
    out_piece = reduce_plane(out_grads[:half], out_grads[half:], BITS_A, ndp)
    out_state = finish([out_piece[k * part : (k + 1) * part] for k in range(nmp)], BITS_A)
    qkv_state = finish(qkv_grads, BITS_B)

    def unpack(kernel, state, idx, shape):
        return call(
            kernel,
            sds(shape, F32),
            bytes_accessed=2 * 4 * math.prod(shape),
            in_specs=[smem, vmem],
            out_specs=vmem,
        )(idx, state)

    up_weight_grad = unpack(unpack_kernel, up_state, idx_a, (1, width, units))[0]
    down_weight_grad = unpack(unpack_rows_kernel, down_state, idx_b, (units, width))
    out_weight_grad = unpack(unpack_rows_kernel, out_state, idx_a, (e, width))
    qkv_weight_grad = unpack(unpack_kernel, qkv_state, idx_b, (3, width, e))

    head_sum = jnp.sum(sum(head_stats), axis=-1)
    copied = jnp.concatenate(
        [mid_stats[:4].reshape(-1), n1_stats[:2].reshape(-1), head_sum.reshape(-1)]
    )
    own_parts = [
        jnp.concatenate([qkvb_grads[k], jnp.take(ub_grads[k], idx_a, axis=0).reshape(-1)])
        for k in range(nmp)
    ]
    small = jnp.concatenate([copied] + own_parts)
    bit = 1
    while bit < ndp:
        small = small + swap_plane(small, bit, ndp)
        bit *= 2
    nc = copied.shape[0]
    no = own_parts[0].shape[0]
    small_sum = small[: nc + no]
    for k in range(1, nmp):
        sent = jnp.concatenate([small[:nc], small[nc + k * no : nc + (k + 1) * no]])
        small_sum = small_sum + to_slot(sent, k, nmp)
    rows_of = small_sum[: 6 * width].reshape(6, width)
    heads_of = small_sum[6 * width : nc].reshape(3, DH)
    qkv_bias_grad = small_sum[nc : nc + 3 * e].reshape(3, e)
    up_bias_grad = small_sum[nc + 3 * e :]
    return (
        block_out,
        input_grad,
        qkv_weight_grad,
        qkv_bias_grad,
        out_weight_grad,
        rows_of[2],
        up_weight_grad,
        up_bias_grad,
        down_weight_grad,
        rows_of[3],
        rows_of[4],
        rows_of[5],
        heads_of[0],
        heads_of[1],
        heads_of[2],
        rows_of[0],
        rows_of[1],
    )


def solution(mesh):
    in_specs = (
        P("dp", None),
        P("dp"),
        P(None, None, "mp"),
        P(None, "mp"),
        P("mp", None),
        P(),
        P(None, "mp"),
        P("mp"),
        P("mp", None),
        P(),
        P(),
        P(),
        P(),
        P(),
        P(),
        P(),
        P(),
        P("dp", None),
    )
    out_specs = (
        P(("dp", "mp"), None),
        P(("dp", "mp"), None),
        P(None, None, "mp"),
        P(None, "mp"),
        P("mp", None),
        P(),
        P(None, "mp"),
        P("mp"),
        P("mp", None),
        P(),
        P(),
        P(),
        P(),
        P(),
        P(),
        P(),
        P(),
    )
    return jax.shard_map(shards, mesh=mesh, in_specs=in_specs, out_specs=out_specs, check_vma=False)
```

time: 945 us -> 722 us (0.76)
  waiting for transfers between devices: 590 us -> 311 us
  Pallas kernels: 0 us -> 170 us
  starting transfers between devices: 0.38 us -> 124 us
  matrix products: 121 us -> 0 us
  blocking collectives: 69 us -> 0 us
  other arithmetic: 91 us -> 57.4 us
  between operations: 15 us -> 2.3 us
    psum x3 -> x0, waiting for transfers between devices: 551 us -> none  [the longest x1 226 us: shards(): lax.psum(jnp.dot(mixture_rows, out_weight, preferred_element_type=jnp.flo...]
    ppermute x0 -> x109, waiting for transfers between devices: none -> 311 us  [the longest x81 243 us: swap_plane(): return lax.ppermute(a, 'dp', [(d, d ^ bit) for d in range(size)])]
    pallas_call x0 -> x21, Pallas kernels: none -> 170 us  [the longest x4 51.6 us: shards(): call(functools.partial(attn_bwd_kernel, first), (sds((PIECES, 3 * part, w...]
    ppermute x0 -> x109, starting transfers between devices: none -> 124 us  [the longest x81 56.2 us: swap_plane(): return lax.ppermute(a, 'dp', [(d, d ^ bit) for d in range(size)])]
    dot_general x25 -> x0, matrix products: 118 us -> none  [the longest x1 19.1 us: shards(): jnp.dot(cotangent, down_weight.T, preferred_element_type=jnp.float32)]
    psum x2 -> x0, blocking collectives: 69 us -> none  [the longest x1 43.8 us: shards(): lax.psum((norm1_gain_grad, norm1_shift_grad, query_gain_grad, query_shift...]
    reduce_sum x17 -> x5, other arithmetic: 46.3 us -> 4.73 us  [the longest x4 3.73 us: shards(): qkvb_grads.append(jnp.sum(gb, axis=1))]
    reduce_scatter x2 -> x0, waiting for transfers between devices: 39.2 us -> none  [the longest x1 39.2 us: shards(): lax.psum_scatter(grad_input_part, 'mp', scatter_dimension=0, tiled=True)]
  transfers between devices with their start and end apart: 5 -> 109, of which waited for: 4 -> 39; matrix products, arithmetic and copies ran while one was open for 13% -> 12% of each run, Pallas kernels for 0% -> 19%
where the time goes in v1:
time: 722 us; the launch traced here: 716 us
  waiting for transfers between devices  311 us (43%)
  Pallas kernels  170 us (24%)
  starting transfers between devices  124 us (17%)
  other arithmetic  57.4 us (8%)
  local copies, waits for them, and re-layouts  51.4 us (7%)
    ppermute x81, waiting for transfers between devices, swap_plane(): return lax.ppermute(a, 'dp', [(d, d ^ bit) for d in range(size)])  243 us
    ppermute x81, starting transfers between devices, swap_plane(): return lax.ppermute(a, 'dp', [(d, d ^ bit) for d in range(size)])  56.2 us
    pallas_call x4, Pallas kernels, shards(): call(functools.partial(attn_bwd_kernel, first), (sds((PIECES, 3 * part, w...  51.6 us
    pallas_call x4, Pallas kernels, shards(): call(functools.partial(mlp_kernel, first), (sds((share, width), F32), sds...  49.3 us
    ppermute x15, starting transfers between devices, to_slot(): return lax.ppermute(a, 'mp', [(s, (s + k) % size) for s in range(size)])  40 us
    ppermute x12, waiting for transfers between devices, from_slot(): return lax.ppermute(a, 'mp', [(s, (s - k) % size) for s in range(size)])  36.1 us
    ppermute x15, waiting for transfers between devices, to_slot(): return lax.ppermute(a, 'mp', [(s, (s + k) % size) for s in range(size)])  31.6 us
    pallas_call x4, Pallas kernels, shards(): call(attn_fwd_kernel, (sds((e, share), F32), sds((e, full), F32), sds((e,...  24.9 us
  transfers between devices with their start and end apart: 109, of which 39 were waited for; matrix products, arithmetic and copies ran while one was open for 12% of the time, Pallas kernels for 19%

profile of v1, /device:TPU:0, one launch (start us, length us, event | category | flops | bytes accessed | tf_op | source)
XLA Modules:
  0.0 715.5 jit_solution(7829560624085042618)
XLA Ops:
  32.6 6.2 shard_map.306
  61.1 30.0 %collective-permute-done.23 = f32[96,768]{1,0:T(8,128)S(1)} collective-permute-done((f32[96,768]{1,0:T(8,128)S(1)}, f32[96,768]{1,0:T(8,128)S(1)}, u32[]{:S(2)}, u32[]{:S(2)}) %collective-permute-start.23) | collective-permute-done | bytes 294944 | tf_op jit(solution)/shard_map/ppermute | solution.py:352
  124.9 11.0 %collective-permute-done.20 = f32[1,96,768]{2,1,0:T(8,128)S(1)} collective-permute-done((f32[1,96,768]{2,1,0:T(8,128)}, f32[1,96,768]{2,1,0:T(8,128)S(1)}, u32[]{:S(2)}, u32[]{:S(2)}) %collective-permute-start.20) | collective-permute-done | bytes 294944 | tf_op jit(solution)/shard_map/ppermute | solution.py:360
  140.6 7.9 %collective-permute-done.2 = f32[2,96,768]{2,1,0:T(8,128)S(1)} collective-permute-done((f32[2,96,768]{2,1,0:T(8,128)S(1)}, f32[2,96,768]{2,1,0:T(8,128)S(1)}, u32[]{:S(2)}, u32[]{:S(2)}) %collective-permute-start.2) | collective-permute-done | bytes 589856 | tf_op jit(solution)/shard_map/ppermute | solution.py:360
  148.6 12.5 %collective-permute-done.33 = f32[2,96,768]{2,1,0:T(8,128)S(1)} collective-permute-done((f32[2,96,768]{2,1,0:T(8,128)S(1)}, f32[2,96,768]{2,1,0:T(8,128)S(1)}, u32[]{:S(2)}, u32[]{:S(2)}) %collective-permute-start.33) | collective-permute-done | bytes 589856 | tf_op jit(solution)/shard_map/ppermute | solution.py:360
  163.8 7.8 %collective-permute-done.25 = f32[2,96,768]{2,1,0:T(8,128)S(1)} collective-permute-done((f32[2,96,768]{2,1,0:T(8,128)S(1)}, f32[2,96,768]{2,1,0:T(8,128)S(1)}, u32[]{:S(2)}, u32[]{:S(2)}) %collective-permute-start.25) | collective-permute-done | bytes 589856 | tf_op jit(solution)/shard_map/ppermute | solution.py:360
  173.8 7.4 %collective-permute-done.17 = f32[2,96,768]{2,1,0:T(8,128)S(1)} collective-permute-done((f32[2,96,768]{2,1,0:T(8,128)S(1)}, f32[2,96,768]{2,1,0:T(8,128)S(1)}, u32[]{:S(2)}, u32[]{:S(2)}) %collective-permute-start.17) | collective-permute-done | bytes 589856 | tf_op jit(solution)/shard_map/ppermute | solution.py:360
  193.0 6.2 shard_map.309
  199.2 6.2 shard_map.307
  205.4 6.2 shard_map.308
  212.1 8.3 %shard_map.310 = (f32[512,768]{1,0:T(8,128)}, bf16[512,768]{1,0:T(8,128)(2,1)}, bf16[4,192,768]{2,1,0:T(8,128)(2,1)}) custom-call(s32[4]{0:T(128)} %compare_select_fusion.1.blk_ref, s32[8]{0:T(128)} %iota.30.refs_0_, s32[8]{0:T(128)} %fusion.32.idx_ref.refs_1_.refs_3_, s32[8]{0:T(128)} %fusion.34.idx_ref.refs_2_, s32[8]{0:T(128)} %fusion.32.idx_ref.refs_1_.refs_3_, ...), custom_call_target="tpu_custom_call" | custom-call | flops 603979776 | bytes 16000000 | tf_op jit(solution)/shard_map/pallas_call | solution.py:547
  221.0 11.3 %shard_map.311 = (f32[512,768]{1,0:T(8,128)}, f32[512,768]{1,0:T(8,128)}, f32[4,96,768]{2,1,0:T(8,128)}, f32[4,96,768]{2,1,0:T(8,128)}, f32[4,96,768]{2,1,0:T(8,...) custom-call(bf16[512,768]{1,0:T(8,128)(2,1)} %get-tuple-element.107.refs_0_, ...), custom_call_target="tpu_custom_call" | custom-call | flops 3623878656 | bytes 16000000 | tf_op jit(solution)/shard_map/pallas_call | solution.py:599
  232.4 12.6 %shard_map.312 = (f32[512,768]{1,0:T(8,128)}, f32[512,768]{1,0:T(8,128)}, f32[4,96,768]{2,1,0:T(8,128)}, f32[4,96,768]{2,1,0:T(8,128)}, f32[4,96,768]{2,1,0:T(8,...) custom-call(bf16[512,768]{1,0:T(8,128)(2,1)} %get-tuple-element.107., ...), custom_call_target="tpu_custom_call", output_to_operand_aliasing={{0}: (8, {}), {1}: (9, {})} | custom-call | flops 3623878656 | bytes 16000000 | tf_op jit(solution)/shard_map/pallas_call | solution.py:599
  245.0 12.6 %shard_map.313 = (f32[512,768]{1,0:T(8,128)}, f32[512,768]{1,0:T(8,128)}, f32[4,96,768]{2,1,0:T(8,128)}, f32[4,96,768]{2,1,0:T(8,128)}, f32[4,96,768]{2,1,0:T(8,...) custom-call(bf16[512,768]{1,0:T(8,128)(2,1)} %get-tuple-element.107., ...), custom_call_target="tpu_custom_call", output_to_operand_aliasing={{0}: (8, {}), {1}: (9, {})} | custom-call | flops 3623878656 | bytes 16000000 | tf_op jit(solution)/shard_map/pallas_call | solution.py:599
  260.9 12.7 %shard_map.314 = (f32[512,768]{1,0:T(8,128)}, f32[512,768]{1,0:T(8,128)}, f32[4,96,768]{2,1,0:T(8,128)}, f32[4,96,768]{2,1,0:T(8,128)}, f32[4,96,768]{2,1,0:T(8,...) custom-call(bf16[512,768]{1,0:T(8,128)(2,1)} %get-tuple-element.107., ...), custom_call_target="tpu_custom_call", output_to_operand_aliasing={{0}: (8, {}), {1}: (9, {})} | custom-call | flops 3623878656 | bytes 16000000 | tf_op jit(solution)/shard_map/pallas_call | solution.py:599
  275.5 8.0 %shard_map.315 = (bf16[512,768]{1,0:T(8,128)(2,1)}, f32[512,768]{1,0:T(8,128)}, bf16[4,192,512]{2,1,0:T(8,128)(2,1)}, f32[8,96,768]{2,1,0:T(8,128)}, f32[8,768]{1,0:T(8,128)}) custom-call(s32[8]{0:T(128)} %fusion.32.idx_ref.refs_1_.refs_3_, f32[512,768]{1,0:T(8,128)} %get-tuple-element.106.mid_ref, f32[512,768]{1,0:T(8,128)} %get-tuple-element.114.acc_ref, ...), custom_call_target="tpu_custom_call" | custom-call | flops 1207959552 | bytes 12000000 | tf_op jit(solution)/shard_map/pallas_call | solution.py:628
  285.6 11.9 %shard_map.316 = (f32[8,72,768]{2,1,0:T(8,128)}, f32[1024,768]{1,0:T(8,128)}, f32[3,64,128]{2,1,0:T(8,128)}, f32[576,128]{1,0:T(8,128)}) custom-call(s32[8]{0:T(128)} %fusion.34.idx_ref.refs_2_, bf16[1024,768]{1,0:T(8,128)(2,1)} %shard_map.305.x_ref, f32[192,512]{1,0:T(8,128)} %get-tuple-element.138.qpre_ref, f32[192,1024]{1,0:T(8,128)} %get-tuple-element.139.kpre_ref, ...), custom_call_target="tpu_custom_call" | custom-call | flops 5536481280 | bytes 14000000 | tf_op jit(solution)/shard_map/pallas_call | solution.py:666
  299.7 13.5 %shard_map.317 = (f32[8,72,768]{2,1,0:T(8,128)}, f32[1024,768]{1,0:T(8,128)}, f32[3,64,128]{2,1,0:T(8,128)}, f32[576,128]{1,0:T(8,128)}) custom-call(s32[8]{0:T(128)} %fusion.32.idx_ref.refs_1_.refs_3_, bf16[1024,768]{1,0:T(8,128)(2,1)} %shard_map.305.x_ref, f32[192,512]{1,0:T(8,128)} %get-tuple-element.133.qpre_ref, ...), custom_call_target="tpu_custom_call", output_to_operand_aliasing={{1}: (14, {})} | custom-call | flops 5536481280 | bytes 14000000 | tf_op jit(solution)/shard_map/pallas_call | solution.py:666
  315.8 13.0 %shard_map.318 = (f32[8,72,768]{2,1,0:T(8,128)}, f32[1024,768]{1,0:T(8,128)}, f32[3,64,128]{2,1,0:T(8,128)}, f32[576,128]{1,0:T(8,128)}) custom-call(s32[8]{0:T(128)} %fusion.34.idx_ref.refs_2_, bf16[1024,768]{1,0:T(8,128)(2,1)} %shard_map.305.x_ref, f32[192,512]{1,0:T(8,128)} %get-tuple-element.128.qpre_ref, ...), custom_call_target="tpu_custom_call", output_to_operand_aliasing={{1}: (14, {})} | custom-call | flops 5536481280 | bytes 14000000 | tf_op jit(solution)/shard_map/pallas_call | solution.py:666
  331.4 13.2 %shard_map.319 = (f32[8,72,768]{2,1,0:T(8,128)}, f32[1024,768]{1,0:T(8,128)}, f32[3,64,128]{2,1,0:T(8,128)}, f32[576,128]{1,0:T(8,128)}) custom-call(s32[8]{0:T(128)} %fusion.32.idx_ref.refs_1_.refs_3_, bf16[1024,768]{1,0:T(8,128)(2,1)} %shard_map.305.x_ref, f32[192,512]{1,0:T(8,128)} %get-tuple-element.122.qpre_ref, ...), custom_call_target="tpu_custom_call", output_to_operand_aliasing={{1}: (14, {})} | custom-call | flops 5536481280 | bytes 14000000 | tf_op jit(solution)/shard_map/pallas_call | solution.py:666
  411.9 46.2 %collective-permute-done.45 = f32[1,72,768]{2,1,0:T(8,128)S(1)} collective-permute-done((f32[1,72,768]{2,1,0:T(8,128)S(1)}, f32[1,72,768]{2,1,0:T(8,128)S(1)}, u32[]{:S(2)}, u32[]{:S(2)}) %collective-permute-start.45) | collective-permute-done | bytes 221216 | tf_op jit(solution)/shard_map/ppermute | solution.py:360
  475.7 11.1 %collective-permute-done.74 = f32[2,96,768]{2,1,0:T(8,128)S(1)} collective-permute-done((f32[2,96,768]{2,1,0:T(8,128)S(1)}, f32[2,96,768]{2,1,0:T(8,128)S(1)}, u32[]{:S(2)}, u32[]{:S(2)}) %collective-permute-start.74) | collective-permute-done | bytes 589856 | tf_op jit(solution)/shard_map/ppermute | solution.py:360
  487.4 12.1 %collective-permute-done.77 = f32[2,96,768]{2,1,0:T(8,128)S(1)} collective-permute-done((f32[2,96,768]{2,1,0:T(8,128)S(1)}, f32[2,96,768]{2,1,0:T(8,128)S(1)}, u32[]{:S(2)}, u32[]{:S(2)}) %collective-permute-start.77) | collective-permute-done | bytes 589856 | tf_op jit(solution)/shard_map/ppermute | solution.py:360
  501.8 10.3 %collective-permute-done.81 = f32[2,96,768]{2,1,0:T(8,128)S(1)} collective-permute-done((f32[2,96,768]{2,1,0:T(8,128)S(1)}, f32[2,96,768]{2,1,0:T(8,128)S(1)}, u32[]{:S(2)}, u32[]{:S(2)}) %collective-permute-start.81) | collective-permute-done | bytes 589856 | tf_op jit(solution)/shard_map/ppermute | solution.py:360
  516.7 8.1 %collective-permute-done.85 = f32[2,96,768]{2,1,0:T(8,128)S(1)} collective-permute-done((f32[2,96,768]{2,1,0:T(8,128)S(1)}, f32[2,96,768]{2,1,0:T(8,128)S(1)}, u32[]{:S(2)}, u32[]{:S(2)}) %collective-permute-start.85) | collective-permute-done | bytes 589856 | tf_op jit(solution)/shard_map/ppermute | solution.py:360
  524.8 14.5 %collective-permute-done.42 = f32[1,72,768]{2,1,0:T(8,128)S(1)} collective-permute-done((f32[1,72,768]{2,1,0:T(8,128)S(1)}, f32[1,72,768]{2,1,0:T(8,128)S(1)}, u32[]{:S(2)}, u32[]{:S(2)}) %collective-permute-start.42) | collective-permute-done | bytes 221216 | tf_op jit(solution)/shard_map/ppermute | solution.py:360
  544.0 24.3 %collective-permute-done.55 = f32[1,72,768]{2,1,0:T(8,128)S(1)} collective-permute-done((f32[1,72,768]{2,1,0:T(8,128)S(1)}, f32[1,72,768]{2,1,0:T(8,128)S(1)}, u32[]{:S(2)}, u32[]{:S(2)}) %collective-permute-start.55) | collective-permute-done | bytes 221216 | tf_op jit(solution)/shard_map/ppermute | solution.py:360
  599.4 8.7 %collective-permute-done.101 = f32[96,768]{1,0:T(8,128)S(1)} collective-permute-done((f32[96,768]{1,0:T(8,128)S(1)}, f32[96,768]{1,0:T(8,128)S(1)}, u32[]{:S(2)}, u32[]{:S(2)}) %collective-permute-start.101) | collective-permute-done | bytes 294944 | tf_op jit(solution)/shard_map/ppermute | solution.py:356
  611.2 8.4 %collective-permute-start.39 = (f32[512,768]{1,0:T(8,128)}, f32[512,768]{1,0:T(8,128)}, u32[]{:S(2)}, u32[]{:S(2)}) collective-permute-start(f32[512,768]{1,0:T(8,128)} %slice.442), channel_id=1, source_target_pairs={{0,1},{1,0},{2,3},{3,2},{4,5},{5,4},{6,7},{7,6},{8,9},{9,8},{10,11... | collective-permute-start | bytes 4718600 | tf_op jit(solution)/shard_map/ppermute | solution.py:689
  635.9 16.8 %collective-permute-done.67 = f32[24,768]{1,0:T(8,128)S(1)} collective-permute-done((f32[24,768]{1,0:T(8,128)S(1)}, f32[24,768]{1,0:T(8,128)S(1)}, u32[]{:S(2)}, u32[]{:S(2)}) %collective-permute-start.67) | collective-permute-done | bytes 73760 | tf_op jit(solution)/shard_map/ppermute | solution.py:356
  656.0 7.4 %collective-permute-done.70 = f32[1,24,768]{2,1,0:T(8,128)S(1)} collective-permute-done((f32[1,24,768]{2,1,0:T(8,128)S(1)}, f32[1,24,768]{2,1,0:T(8,128)S(1)}, u32[]{:S(2)}, u32[]{:S(2)}) %collective-permute-start.70) | collective-permute-done | bytes 73760 | tf_op jit(solution)/shard_map/ppermute | solution.py:360
  664.4 6.9 collective-permute-start.62
  (527 shorter events, 319.7 us)
Async XLA Ops:
  4.5 47.6 %collective-permute-start.10 = (f32[96,768]{1,0:T(8,128)}, f32[96,768]{1,0:T(8,128)}, u32[]{:S(2)}, u32[]{:S(2)}) collective-permute-start(f32[96,768]{1,0:T(8,128)} %dynamic-slice_bitcast_fusion), channel_id=1, source_target_pairs={{0,1},{1,2},{2,3},{3,0},{4,5},{5,6},{6,7},{7,4},{8,9},{9,10},{10,1... | collective-permute-start | bytes 884744 | tf_op jit(solution)/shard_map/ppermute | solution.py:352
  7.5 44.7 %collective-permute-start.5 = (f32[96,768]{1,0:T(8,128)}, f32[96,768]{1,0:T(8,128)S(1)}, u32[]{:S(2)}, u32[]{:S(2)}) collective-permute-start(f32[96,768]{1,0:T(8,128)} %dynamic-slice_bitcast_fusion), channel_id=1, source_target_pairs={{0,2},{1,3},{2,0},{3,1},{4,6},{5,7},{6,4},{7,5},{8,10},{9,11},{10,... | collective-permute-start | bytes 884744 | tf_op jit(solution)/shard_map/ppermute | solution.py:352
  13.7 41.4 %collective-permute-start = (f32[96,768]{1,0:T(8,128)}, f32[96,768]{1,0:T(8,128)}, u32[]{:S(2)}, u32[]{:S(2)}) collective-permute-start(f32[96,768]{1,0:T(8,128)} %dynamic-slice_bitcast_fusion), channel_id=1, source_target_pairs={{0,3},{1,0},{2,1},{3,2},{4,7},{5,4},{6,5},{7,6},{8,11},{9,8},{10,9... | collective-permute-start | bytes 884744 | tf_op jit(solution)/shard_map/ppermute | solution.py:352
  52.1 39.0 %collective-permute-start.23 = (f32[96,768]{1,0:T(8,128)S(1)}, f32[96,768]{1,0:T(8,128)S(1)}, u32[]{:S(2)}, u32[]{:S(2)}) collective-permute-start(f32[96,768]{1,0:T(8,128)S(1)} %get-tuple-element.256), channel_id=1, source_target_pairs={{0,2},{1,3},{2,0},{3,1},{4,6},{5,7},{6,4},{7,5},{8,10},{9,11},{10,... | collective-permute-start | bytes 884744 | tf_op jit(solution)/shard_map/ppermute | solution.py:352
  52.2 42.1 %collective-permute-start.27 = (f32[96,768]{1,0:T(8,128)S(1)}, f32[96,768]{1,0:T(8,128)S(1)}, u32[]{:S(2)}, u32[]{:S(2)}) collective-permute-start(f32[96,768]{1,0:T(8,128)S(1)} %get-tuple-element.247), channel_id=1, source_target_pairs={{0,2},{1,3},{2,0},{3,1},{4,6},{5,7},{6,4},{7,5},{8,10},{9,11},{10,... | collective-permute-start | bytes 884744 | tf_op jit(solution)/shard_map/ppermute | solution.py:352
  55.1 40.6 %collective-permute-start.15 = (f32[96,768]{1,0:T(8,128)S(1)}, f32[96,768]{1,0:T(8,128)}, u32[]{:S(2)}, u32[]{:S(2)}) collective-permute-start(f32[96,768]{1,0:T(8,128)S(1)} %get-tuple-element.256), channel_id=1, source_target_pairs={{0,1},{1,2},{2,3},{3,0},{4,5},{5,6},{6,7},{7,4},{8,9},{9,10},{10,1... | collective-permute-start | bytes 884744 | tf_op jit(solution)/shard_map/ppermute | solution.py:352
  55.1 41.2 %collective-permute-start.19 = (f32[96,768]{1,0:T(8,128)S(1)}, f32[96,768]{1,0:T(8,128)}, u32[]{:S(2)}, u32[]{:S(2)}) collective-permute-start(f32[96,768]{1,0:T(8,128)S(1)} %get-tuple-element.247), channel_id=1, source_target_pairs={{0,1},{1,2},{2,3},{3,0},{4,5},{5,6},{6,7},{7,4},{8,9},{9,10},{10,1... | collective-permute-start | bytes 884744 | tf_op jit(solution)/shard_map/ppermute | solution.py:352
  59.6 44.9 %collective-permute-start.11 = (f32[1,96,768]{2,1,0:T(8,128)}, f32[1,96,768]{2,1,0:T(8,128)S(1)}, u32[]{:S(2)}, u32[]{:S(2)}) collective-permute-start(f32[1,96,768]{2,1,0:T(8,128)} %bitcast.13), channel_id=1, source_target_pairs={{0,8},{4,12},{8,0},{12,4},{16,24},{20,28},{24,16},{28,20},{1,9},{5... | collective-permute-start | bytes 884744 | tf_op jit(solution)/shard_map/ppermute | solution.py:360
  122.6 38.6 %collective-permute-start.33 = (f32[2,96,768]{2,1,0:T(8,128)S(1)}, f32[2,96,768]{2,1,0:T(8,128)S(1)}, u32[]{:S(2)}, u32[]{:S(2)}) collective-permute-start(f32[2,96,768]{2,1,0:T(8,128)S(1)} %pad_maximum_fusion.25), channel_id=1, source_target_pairs={{0,16},{4,20},{8,24},{12,28},{16,0},{20,4},{24,8},{28,12},{1,17},{... | collective-permute-start | bytes 1769480 | tf_op jit(solution)/shard_map/ppermute | solution.py:360
  148.6 37.3 %collective-permute-start.13 = (f32[4,96,768]{2,1,0:T(8,128)S(1)}, f32[4,96,768]{2,1,0:T(8,128)S(1)}, u32[]{:S(2)}, u32[]{:S(2)}) collective-permute-start(f32[4,96,768]{2,1,0:T(8,128)S(1)} %pad_maximum_fusion.8), channel_id=1, source_target_pairs={{0,4},{4,0},{8,12},{12,8},{16,20},{20,16},{24,28},{28,24},{1,5},{5... | collective-permute-start | bytes 3538952 | tf_op jit(solution)/shard_map/ppermute | solution.py:360
  181.2 39.3 %collective-permute-start.34 = (f32[4,96,768]{2,1,0:T(8,128)S(1)}, f32[4,96,768]{2,1,0:T(8,128)}, u32[]{:S(2)}, u32[]{:S(2)}) collective-permute-start(f32[4,96,768]{2,1,0:T(8,128)S(1)} %pad_maximum_fusion.13.refs_2_), channel_id=1, source_target_pairs={{0,4},{4,0},{8,12},{12,8},{16,20},{20,16},{24,28},{28,24},{1,5},{5... | collective-permute-start | bytes 3538952 | tf_op jit(solution)/shard_map/ppermute | solution.py:360
  183.2 49.2 %collective-permute-start.38 = (f32[4,96,768]{2,1,0:T(8,128)S(1)}, f32[4,96,768]{2,1,0:T(8,128)}, u32[]{:S(2)}, u32[]{:S(2)}) collective-permute-start(f32[4,96,768]{2,1,0:T(8,128)S(1)} %pad_maximum_fusion.14.refs_6_), channel_id=1, source_target_pairs={{0,4},{4,0},{8,12},{12,8},{16,20},{20,16},{24,28},{28,24},{1,5},{5... | collective-permute-start | bytes 3538952 | tf_op jit(solution)/shard_map/ppermute | solution.py:360
  185.8 59.2 %collective-permute-start.26 = (f32[4,96,768]{2,1,0:T(8,128)S(1)}, f32[4,96,768]{2,1,0:T(8,128)}, u32[]{:S(2)}, u32[]{:S(2)}) collective-permute-start(f32[4,96,768]{2,1,0:T(8,128)S(1)} %pad_maximum_fusion.11.refs_2_), channel_id=1, source_target_pairs={{0,4},{4,0},{8,12},{12,8},{16,20},{20,16},{24,28},{28,24},{1,5},{5... | collective-permute-start | bytes 3538952 | tf_op jit(solution)/shard_map/ppermute | solution.py:360
  188.4 56.6 %collective-permute-start.30 = (f32[4,96,768]{2,1,0:T(8,128)S(1)}, f32[4,96,768]{2,1,0:T(8,128)}, u32[]{:S(2)}, u32[]{:S(2)}) collective-permute-start(f32[4,96,768]{2,1,0:T(8,128)S(1)} %pad_maximum_fusion.12.refs_6_), channel_id=1, source_target_pairs={{0,4},{4,0},{8,12},{12,8},{16,20},{20,16},{24,28},{28,24},{1,5},{5... | collective-permute-start | bytes 3538952 | tf_op jit(solution)/shard_map/ppermute | solution.py:360
  190.4 69.0 %collective-permute-start.18 = (f32[4,96,768]{2,1,0:T(8,128)}, f32[4,96,768]{2,1,0:T(8,128)S(1)}, u32[]{:S(2)}, u32[]{:S(2)}) collective-permute-start(f32[4,96,768]{2,1,0:T(8,128)} %pad_maximum_fusion.9.refs_2_), channel_id=1, source_target_pairs={{0,4},{4,0},{8,12},{12,8},{16,20},{20,16},{24,28},{28,24},{1,5},{5... | collective-permute-start | bytes 3538952 | tf_op jit(solution)/shard_map/ppermute | solution.py:360
  220.5 39.0 %collective-permute-start.22 = (f32[4,96,768]{2,1,0:T(8,128)}, f32[4,96,768]{2,1,0:T(8,128)S(1)}, u32[]{:S(2)}, u32[]{:S(2)}) collective-permute-start(f32[4,96,768]{2,1,0:T(8,128)} %pad_maximum_fusion.10.refs_6_), channel_id=1, source_target_pairs={{0,4},{4,0},{8,12},{12,8},{16,20},{20,16},{24,28},{28,24},{1,5},{5... | collective-permute-start | bytes 3538952 | tf_op jit(solution)/shard_map/ppermute | solution.py:360
  299.7 65.5 %collective-permute-start.40 = (f32[4,72,768]{2,1,0:T(8,128)}, f32[4,72,768]{2,1,0:T(8,128)}, u32[]{:S(2)}, u32[]{:S(2)}) collective-permute-start(f32[4,72,768]{2,1,0:T(8,128)} %slice.444), channel_id=1, source_target_pairs={{0,4},{4,0},{8,12},{12,8},{16,20},{20,16},{24,28},{28,24},{1,5},{5... | collective-permute-start | bytes 2654216 | tf_op jit(solution)/shard_map/ppermute | solution.py:360
  315.4 50.4 %collective-permute-start.43 = (f32[4,72,768]{2,1,0:T(8,128)}, f32[4,72,768]{2,1,0:T(8,128)}, u32[]{:S(2)}, u32[]{:S(2)}) collective-permute-start(f32[4,72,768]{2,1,0:T(8,128)} %slice.450), channel_id=1, source_target_pairs={{0,4},{4,0},{8,12},{12,8},{16,20},{20,16},{24,28},{28,24},{1,5},{5... | collective-permute-start | bytes 2654216 | tf_op jit(solution)/shard_map/ppermute | solution.py:360
  331.4 35.7 %collective-permute-start.47 = (f32[4,72,768]{2,1,0:T(8,128)}, f32[4,72,768]{2,1,0:T(8,128)}, u32[]{:S(2)}, u32[]{:S(2)}) collective-permute-start(f32[4,72,768]{2,1,0:T(8,128)} %slice.456), channel_id=1, source_target_pairs={{0,4},{4,0},{8,12},{12,8},{16,20},{20,16},{24,28},{28,24},{1,5},{5... | collective-permute-start | bytes 2654216 | tf_op jit(solution)/shard_map/ppermute | solution.py:360
  393.5 77.6 %collective-permute-start.92 = (f32[2,96,768]{2,1,0:T(8,128)S(1)}, f32[2,96,768]{2,1,0:T(8,128)S(1)}, u32[]{:S(2)}, u32[]{:S(2)}) collective-permute-start(f32[2,96,768]{2,1,0:T(8,128)S(1)} %slice.599), channel_id=1, source_target_pairs={{0,8},{4,12},{8,0},{12,4},{16,24},{20,28},{24,16},{28,20},{1,9},{5... | collective-permute-start | bytes 1769480 | tf_op jit(solution)/shard_map/ppermute | solution.py:360
  394.9 77.9 %collective-permute-start.95 = (f32[2,96,768]{2,1,0:T(8,128)S(1)}, f32[2,96,768]{2,1,0:T(8,128)S(1)}, u32[]{:S(2)}, u32[]{:S(2)}) collective-permute-start(f32[2,96,768]{2,1,0:T(8,128)S(1)} %slice.603), channel_id=1, source_target_pairs={{0,8},{4,12},{8,0},{12,4},{16,24},{20,28},{24,16},{28,20},{1,9},{5... | collective-permute-start | bytes 1769480 | tf_op jit(solution)/shard_map/ppermute | solution.py:360
  402.0 71.4 %collective-permute-start.99 = (f32[2,96,768]{2,1,0:T(8,128)S(1)}, f32[2,96,768]{2,1,0:T(8,128)S(1)}, u32[]{:S(2)}, u32[]{:S(2)}) collective-permute-start(f32[2,96,768]{2,1,0:T(8,128)S(1)} %slice.607), channel_id=1, source_target_pairs={{0,8},{4,12},{8,0},{12,4},{16,24},{20,28},{24,16},{28,20},{1,9},{5... | collective-permute-start | bytes 1769480 | tf_op jit(solution)/shard_map/ppermute | solution.py:360
  403.6 71.5 %collective-permute-start.103 = (f32[2,96,768]{2,1,0:T(8,128)S(1)}, f32[2,96,768]{2,1,0:T(8,128)S(1)}, u32[]{:S(2)}, u32[]{:S(2)}) collective-permute-start(f32[2,96,768]{2,1,0:T(8,128)S(1)} %slice.611), channel_id=1, source_target_pairs={{0,8},{4,12},{8,0},{12,4},{16,24},{20,28},{24,16},{28,20},{1,9},{5... | collective-permute-start | bytes 1769480 | tf_op jit(solution)/shard_map/ppermute | solution.py:360
  410.3 47.7 %collective-permute-start.45 = (f32[1,72,768]{2,1,0:T(8,128)S(1)}, f32[1,72,768]{2,1,0:T(8,128)S(1)}, u32[]{:S(2)}, u32[]{:S(2)}) collective-permute-start(f32[1,72,768]{2,1,0:T(8,128)S(1)} %slice.556), channel_id=1, source_target_pairs={{0,8},{4,12},{8,0},{12,4},{16,24},{20,28},{24,16},{28,20},{1,9},{5... | collective-permute-start | bytes 663560 | tf_op jit(solution)/shard_map/ppermute | solution.py:360
  472.8 39.3 %collective-permute-start.81 = (f32[2,96,768]{2,1,0:T(8,128)S(1)}, f32[2,96,768]{2,1,0:T(8,128)S(1)}, u32[]{:S(2)}, u32[]{:S(2)}) collective-permute-start(f32[2,96,768]{2,1,0:T(8,128)S(1)} %slice.590), channel_id=1, source_target_pairs={{0,16},{4,20},{8,24},{12,28},{16,0},{20,4},{24,8},{28,12},{1,17},{... | collective-permute-start | bytes 1769480 | tf_op jit(solution)/shard_map/ppermute | solution.py:360
  473.4 51.3 %collective-permute-start.85 = (f32[2,96,768]{2,1,0:T(8,128)S(1)}, f32[2,96,768]{2,1,0:T(8,128)S(1)}, u32[]{:S(2)}, u32[]{:S(2)}) collective-permute-start(f32[2,96,768]{2,1,0:T(8,128)S(1)} %slice.594), channel_id=1, source_target_pairs={{0,16},{4,20},{8,24},{12,28},{16,0},{20,4},{24,8},{28,12},{1,17},{... | collective-permute-start | bytes 1769480 | tf_op jit(solution)/shard_map/ppermute | solution.py:360
  475.1 68.4 %collective-permute-start.65 = (f32[2,96,768]{2,1,0:T(8,128)S(1)}, f32[2,96,768]{2,1,0:T(8,128)S(1)}, u32[]{:S(2)}, u32[]{:S(2)}) collective-permute-start(f32[2,96,768]{2,1,0:T(8,128)S(1)} %slice.573), channel_id=1, source_target_pairs={{0,16},{4,20},{8,24},{12,28},{16,0},{20,4},{24,8},{28,12},{1,17},{... | collective-permute-start | bytes 1769480 | tf_op jit(solution)/shard_map/ppermute | solution.py:360
  486.8 52.5 %collective-permute-start.42 = (f32[1,72,768]{2,1,0:T(8,128)S(1)}, f32[1,72,768]{2,1,0:T(8,128)S(1)}, u32[]{:S(2)}, u32[]{:S(2)}) collective-permute-start(f32[1,72,768]{2,1,0:T(8,128)S(1)} %slice.552), channel_id=1, source_target_pairs={{0,16},{4,20},{8,24},{12,28},{16,0},{20,4},{24,8},{28,12},{1,17},{... | collective-permute-start | bytes 663560 | tf_op jit(solution)/shard_map/ppermute | solution.py:360
  499.5 40.2 %collective-permute-start.46 = (f32[72,768]{1,0:T(8,128)S(1)}, f32[72,768]{1,0:T(8,128)S(1)}, u32[]{:S(2)}, u32[]{:S(2)}) collective-permute-start(f32[72,768]{1,0:T(8,128)S(1)} %fusion.19), channel_id=1, source_target_pairs={{0,1},{1,2},{2,3},{3,0},{4,5},{5,6},{6,7},{7,4},{8,9},{9,10},{10,1... | collective-permute-start | bytes 663560 | tf_op jit(solution)/shard_map/ppermute | solution.py:356
  539.3 51.6 %collective-permute-start.93 = (f32[1,96,768]{2,1,0:T(8,128)S(1)}, f32[1,96,768]{2,1,0:T(8,128)S(1)}, u32[]{:S(2)}, u32[]{:S(2)}) collective-permute-start(f32[1,96,768]{2,1,0:T(8,128)S(1)} %slice.601), channel_id=1, source_target_pairs={{0,16},{4,20},{8,24},{12,28},{16,0},{20,4},{24,8},{28,12},{1,17},{... | collective-permute-start | bytes 884744 | tf_op jit(solution)/shard_map/ppermute | solution.py:360
  611.2 73.5 %collective-permute-start.39 = (f32[512,768]{1,0:T(8,128)}, f32[512,768]{1,0:T(8,128)}, u32[]{:S(2)}, u32[]{:S(2)}) collective-permute-start(f32[512,768]{1,0:T(8,128)} %slice.442), channel_id=1, source_target_pairs={{0,1},{1,0},{2,3},{3,2},{4,5},{5,4},{6,7},{7,6},{8,9},{9,8},{10,11... | collective-permute-start | bytes 4718600 | tf_op jit(solution)/shard_map/ppermute | solution.py:689
  619.8 44.7 %collective-permute-start.56 = (f32[2,72,768]{2,1,0:T(8,128)S(1)}, f32[2,72,768]{2,1,0:T(8,128)S(1)}, u32[]{:S(2)}, u32[]{:S(2)}) collective-permute-start(f32[2,72,768]{2,1,0:T(8,128)S(1)} %pad_maximum_fusion.34), channel_id=1, source_target_pairs={{0,8},{4,12},{8,0},{12,4},{16,24},{20,28},{24,16},{28,20},{1,9},{5... | collective-permute-start | bytes 1327112 | tf_op jit(solution)/shard_map/ppermute | solution.py:360
  (136 other events, 1901.1 us)

commit v2 on v1

v2 whole, which is shorter than its diff:
```python
import functools
import math

import jax
import jax.numpy as jnp
from jax import lax
from jax.experimental import pallas as pl
from jax.experimental.pallas import tpu as pltpu
from jax.sharding import PartitionSpec as P

F32 = jnp.float32
BF16 = jnp.bfloat16
DH = 64
SEQ_LEN = 1024
NORM_EPS = 1e-06
PIECES = 8
SEG_COLS = 128
LOG2E = math.log2(math.e)
SCALE = DH ** (-0.5)
BITS_A = (2, 4, 1)
BITS_B = (4, 2, 1)
VMEM_LIMIT = 56 * 1024 * 1024


def mm(a, b):
    return lax.dot_general(a, b, (((1,), (0,)), ((), ())), preferred_element_type=F32)


def mm_nt(a, b):
    return lax.dot_general(a, b, (((1,), (1,)), ((), ())), preferred_element_type=F32)


def mm_tn(a, b):
    return lax.dot_general(a, b, (((0,), (0,)), ((), ())), preferred_element_type=F32)


def call(kernel, out_shape, flops=0, bytes_accessed=0, **kw):
    return pl.pallas_call(
        kernel,
        out_shape=out_shape,
        compiler_params=pltpu.CompilerParams(vmem_limit_bytes=VMEM_LIMIT),
        cost_estimate=pl.CostEstimate(
            flops=flops, bytes_accessed=bytes_accessed, transcendentals=0
        ),
        **kw,
    )


def sds(shape, dtype):
    return jax.ShapeDtypeStruct(shape, dtype)


def row_norm(x):
    mean = jnp.mean(x, axis=-1, keepdims=True)
    cen = x - mean
    rstd = lax.rsqrt(jnp.mean(cen * cen, axis=-1, keepdims=True) + NORM_EPS)
    return cen * rstd, rstd


def row_norm_back(f, n, rstd):
    mean_f = jnp.mean(f, axis=-1, keepdims=True)
    mean_fn = jnp.mean(f * n, axis=-1, keepdims=True)
    return (f - mean_f - n * mean_fn) * rstd


def col_norm(x):
    mean = jnp.mean(x, axis=0, keepdims=True)
    cen = x - mean
    rstd = lax.rsqrt(jnp.mean(cen * cen, axis=0, keepdims=True) + NORM_EPS)
    return cen * rstd, rstd


def col_norm_back(f, n, rstd):
    mean_f = jnp.mean(f, axis=0, keepdims=True)
    mean_fn = jnp.mean(f * n, axis=0, keepdims=True)
    return (f - mean_f - n * mean_fn) * rstd


def lane_fold(x):
    out = x[:, :128]
    for t in range(1, x.shape[1] // 128):
        out = out + x[:, t * 128 : (t + 1) * 128]
    return out


def norm1_kernel(blk_ref, x_ref, g_ref, s_ref, out_ref):
    n, _ = row_norm(x_ref[...].astype(F32))
    out_ref[...] = (n * g_ref[...] + s_ref[...]).astype(BF16)


def build_q_aug(q_pre, qg, qs, qaug_ref):
    n, rstd = col_norm(q_pre)
    q_low = (n * qg + qs).astype(BF16)
    scaled = q_low.astype(F32) * (SCALE * LOG2E)
    hi = scaled.astype(BF16)
    lo = (scaled - hi.astype(F32)).astype(BF16)
    qaug_ref[0:DH, :] = hi
    qaug_ref[DH : 2 * DH, :] = lo
    return n, rstd, q_low


def build_k_aug(k_pre, kg, kaug_ref):
    n, rstd = col_norm(k_pre)
    k_low = (n * kg).astype(BF16)
    kaug_ref[:, 0 : 2 * DH] = jnp.concatenate([k_low, k_low], axis=0).T
    return n, rstd, k_low


def attn_fwd_kernel(
    at, ia_ref, ib_ref, x_ref, wa_ref, wb_ref, b_ref, qg_ref, qs_ref, kg_ref, kmask_ref, qhot_ref,
    qpre_ref, kpre_ref, vt_ref, wt_ref, ow_ref, mixt_ref, mixf_ref, l_ref,
    qaug_ref, kaug_ref,
):
    part = 24
    e = PIECES * part
    rows = qhot_ref.shape[1]
    heads = e // DH
    for s, (w_ref, i_ref, off) in enumerate(
        ((wa_ref, ia_ref, 0), (wa_ref, ia_ref, part), (wb_ref, ib_ref, 0), (wb_ref, ib_ref, part))
    ):
        w = jnp.concatenate(
            [w_ref[i_ref[p], at, off : off + part, :] for p in range(PIECES)], axis=0
        ).astype(BF16)
        if s < 3:
            wt_ref[s * e : (s + 1) * e, :] = w
        else:
            ow_ref[...] = w
    qpre_ref[...] = mm_nt(wt_ref[0:e, :], x_ref[0:rows, :]) + b_ref[0:e, :]
    kpre_ref[...] = mm_nt(wt_ref[e : 2 * e, :], x_ref[...]) + b_ref[e : 2 * e, :]
    vt_ref[...] = (mm_nt(wt_ref[2 * e : 3 * e, :], x_ref[...]) + b_ref[2 * e : 3 * e, :]).astype(
        BF16
    )
    qaug_ref[2 * DH :, :] = qhot_ref[...]
    kaug_ref[:, 2 * DH :] = kmask_ref[...]
    ones = jnp.ones((16, x_ref.shape[0]), BF16)
    for h in range(heads):
        hs = slice(h * DH, (h + 1) * DH)
        build_q_aug(qpre_ref[hs, :], qg_ref[...], qs_ref[...], qaug_ref)
        build_k_aug(kpre_ref[hs, :], kg_ref[...], kaug_ref)
        prob = jnp.exp2(mm(kaug_ref[...], qaug_ref[...])).astype(BF16)
        vaug = jnp.concatenate([vt_ref[hs, :], ones], axis=0)
        o = mm(vaug, prob)
        total = o[DH : DH + 1, :]
        l_ref[h : h + 1, :] = total
        mix = o[0:DH, :] / total
        mixf_ref[hs, :] = mix
        mixt_ref[hs, :] = mix.astype(BF16)


def out_norm2_kernel(nslot, blk_ref, x_ref, *refs):
    mixes = refs[:nslot]
    ws = refs[nslot : 2 * nslot]
    ob_ref, g_ref, s_ref, mid_ref, sec_ref = refs[2 * nslot :]
    acc = x_ref[...].astype(F32) + ob_ref[...]
    for k in range(nslot):
        acc = acc + mm_tn(mixes[k][...], ws[k][...])
    mid_ref[...] = acc
    n, _ = row_norm(acc)
    sec_ref[...] = (n * g_ref[...] + s_ref[...]).astype(BF16)


def mlp_kernel(first, *refs):
    if first:
        (sec_ref, cot_ref, ua_ref, ub_ref, ba_ref, bb_ref, da_ref, db_ref) = refs[:8]
        outs = refs[8:]
    else:
        (sec_ref, cot_ref, ua_ref, ub_ref, ba_ref, bb_ref, da_ref, db_ref, acc_in, gs_in) = refs[:10]
        outs = refs[10:]
    (acc_ref, gs_ref, gua_ref, gub_ref, gda_ref, gdb_ref, gba_ref, gbb_ref) = outs
    part = ua_ref.shape[1]
    up = jnp.concatenate([ua_ref[0], ub_ref[0]], axis=0).astype(BF16)
    down = jnp.concatenate([da_ref[0], db_ref[0]], axis=0).astype(BF16)
    bias = jnp.concatenate([ba_ref[0], bb_ref[0]], axis=1)
    sec = sec_ref[...]
    cot = cot_ref[...]
    pre = mm_nt(sec, up) + bias
    cdf = 0.5 * (1.0 + lax.erf(pre * (1.0 / math.sqrt(2.0))))
    hid = (pre * cdf).astype(BF16)
    pdf = jnp.exp(-0.5 * pre * pre) * (1.0 / math.sqrt(2.0 * math.pi))
    gpre_f = mm_nt(cot, down) * (cdf + pre * pdf)
    gpre = gpre_f.astype(BF16)
    gb = jnp.sum(gpre.astype(F32), axis=0, keepdims=True)
    gba_ref[0] = gb[:, :part]
    gbb_ref[0] = gb[:, part:]
    acc_new = mm(hid, down)
    gs_new = mm(gpre, up)
    if first:
        @pl.when(pl.program_id(0) == 0)
        def _():
            acc_ref[...] = acc_new
            gs_ref[...] = gs_new

        @pl.when(pl.program_id(0) > 0)
        def _():
            acc_ref[...] += acc_new
            gs_ref[...] += gs_new
    else:
        @pl.when(pl.program_id(0) == 0)
        def _():
            acc_ref[...] = acc_in[...] + acc_new
            gs_ref[...] = gs_in[...] + gs_new

        @pl.when(pl.program_id(0) > 0)
        def _():
            acc_ref[...] += acc_new
            gs_ref[...] += gs_new
    gd = mm_tn(hid, cot)
    gda_ref[0] = gd[:part]
    gdb_ref[0] = gd[part:]
    gu = mm_tn(gpre, sec)
    gua_ref[0] = gu[:part]
    gub_ref[0] = gu[part:]


def mid_kernel(
    nslot, idx_ref, mid_ref, acc_ref, gs_ref, cot_ref, db_ref, g_ref, *refs
):
    ows = refs[:nslot]
    mixts = refs[nslot : 2 * nslot]
    gmts = refs[2 * nslot : 3 * nslot]
    bo_ref, gm_ref, gow_keep, gow_send, st_ref = refs[3 * nslot :]
    part = 24
    mid = mid_ref[...]
    bo_ref[...] = (mid + acc_ref[...] + db_ref[...]).astype(BF16)
    n, rstd = row_norm(mid)
    e = gs_ref[...]
    cot = cot_ref[...].astype(F32)
    gm = cot + row_norm_back(e * g_ref[...], n, rstd)
    gm_ref[...] = gm
    gm_low = gm.astype(BF16)
    st_ref[0:1, :] = jnp.sum(e * n, axis=0, keepdims=True)
    st_ref[1:2, :] = jnp.sum(e, axis=0, keepdims=True)
    st_ref[2:3, :] = jnp.sum(gm_low.astype(F32), axis=0, keepdims=True)
    st_ref[3:4, :] = jnp.sum(cot, axis=0, keepdims=True)
    st_ref[4:8, :] = jnp.zeros((4, mid.shape[1]), F32)
    for k in range(nslot):
        gmts[k][...] = mm_nt(ows[k][...], gm_low).astype(BF16)
        g = mm(mixts[k][...], gm_low)
        for p in range(PIECES):
            at = idx_ref[p]
            rows = slice(k * part, (k + 1) * part)

            @pl.when(at < PIECES // 2)
            def _():
                gow_keep[at, rows, :] = g[p * part : (p + 1) * part, :]

            @pl.when(at >= PIECES // 2)
            def _():
                gow_send[at - PIECES // 2, rows, :] = g[p * part : (p + 1) * part, :]


def attn_bwd_kernel(
    first, idx_ref, x_ref, qpre_ref, kpre_ref, vt_ref, wt_ref, gmt_ref, mixt_ref, l_ref,
    qg_ref, qs_ref, kg_ref, kmask_ref, qhot_ref, *refs
):
    if first:
        gk_ref, gs_ref, gn_ref, st_ref, gb_ref, qaug_ref, kaug_ref, gpt_ref = refs
    else:
        gn_in, gk_ref, gs_ref, gn_ref, st_ref, gb_ref, qaug_ref, kaug_ref, gpt_ref = refs
    part = 24
    e = PIECES * part
    rows = qhot_ref.shape[1]
    full = x_ref.shape[0]
    heads = e // DH
    qaug_ref[2 * DH :, :] = qhot_ref[...]
    kaug_ref[:, 2 * DH :] = kmask_ref[...]
    qg, qs, kg = qg_ref[...], qs_ref[...], kg_ref[...]
    qg_sum = jnp.zeros((DH, 128), F32)
    qs_sum = jnp.zeros((DH, 128), F32)
    kg_sum = jnp.zeros((DH, 128), F32)
    one_rows = (lax.broadcasted_iota(jnp.int32, (DH, full), 0) < 3).astype(F32).astype(BF16)
    row_no = lax.broadcasted_iota(jnp.int32, (DH, rows), 0)
    for h in range(heads):
        hs = slice(h * DH, (h + 1) * DH)
        qn, qr, q_low = build_q_aug(qpre_ref[hs, :], qg, qs, qaug_ref)
        kn, kr, k_low = build_k_aug(kpre_ref[hs, :], kg, kaug_ref)
        inv = 1.0 / l_ref[h : h + 1, :]
        go = gmt_ref[hs, :].astype(F32) * inv
        go_low = go.astype(BF16)
        delta = -jnp.sum(go_low.astype(F32) * mixt_ref[hs, :], axis=0, keepdims=True)
        d0 = delta.astype(BF16).astype(F32)
        d1 = (delta - d0).astype(BF16).astype(F32)
        d2 = delta - d0 - d1
        extra = jnp.where(
            row_no == 0, d0, jnp.where(row_no == 1, d1, jnp.where(row_no == 2, d2, 0.0))
        ).astype(BF16)
        goaug = jnp.concatenate([go_low, extra], axis=0)
        vaug = jnp.concatenate([vt_ref[hs, :], one_rows], axis=0).T
        prob = jnp.exp2(mm(kaug_ref[...], qaug_ref[...]))
        ds = (prob * mm(vaug, goaug)).astype(BF16)
        gv = mm_nt(go_low, prob.astype(BF16))
        gk = mm_nt(q_low, ds) * SCALE
        gq = mm(k_low, ds) * SCALE
        qg_sum += lane_fold(gq * qn)
        qs_sum += lane_fold(gq)
        kg_sum += lane_fold(gk * kn)
        gpt_ref[h * DH : (h + 1) * DH, 0:rows] = col_norm_back(gq * qg, qn, qr).astype(BF16)
        gpt_ref[e + h * DH : e + (h + 1) * DH, :] = col_norm_back(gk * kg, kn, kr).astype(BF16)
        gpt_ref[2 * e + h * DH : 2 * e + (h + 1) * DH, :] = gv.astype(BF16)
    st_ref[0] = qg_sum
    st_ref[1] = qs_sum
    st_ref[2] = kg_sum
    gpq = gpt_ref[0:e, 0:rows]
    gpkv = gpt_ref[e : 3 * e, :]
    gb_ref[0:e, :] = lane_fold(gpq.astype(F32))
    gb_ref[e : 3 * e, :] = lane_fold(gpkv.astype(F32))
    gwq = mm(gpq, x_ref[0:rows, :])
    gwkv = mm(gpkv, x_ref[...])

    def put(ref, at, p):
        ref[at, 0:part, :] = gwq[p * part : (p + 1) * part, :]
        ref[at, part : 2 * part, :] = gwkv[p * part : (p + 1) * part, :]
        ref[at, 2 * part : 3 * part, :] = gwkv[e + p * part : e + (p + 1) * part, :]

    for p in range(PIECES):
        at = idx_ref[p]

        @pl.when(at < PIECES // 2)
        def _():
            put(gk_ref, at, p)

        @pl.when(at >= PIECES // 2)
        def _():
            put(gs_ref, at - PIECES // 2, p)

    gnq = mm_tn(gpq, wt_ref[0:e, :])
    gnkv = mm_tn(gpkv, wt_ref[e : 3 * e, :])
    if first:
        gn_ref[0:rows, :] = gnkv[0:rows] + gnq
        gn_ref[rows:, :] = gnkv[rows:]
    else:
        gn_ref[0:rows, :] = gn_in[0:rows, :] + gnkv[0:rows] + gnq
        gn_ref[rows:, :] = gn_in[rows:, :] + gnkv[rows:]


def norm1_stats_kernel(blk_ref, x_ref, gn_ref, out_ref):
    n, _ = row_norm(x_ref[...].astype(F32))
    e = gn_ref[...]

    @pl.when(pl.program_id(0) == 0)
    def _():
        out_ref[...] = jnp.zeros_like(out_ref)

    out_ref[0:1, :] += jnp.sum(e * n, axis=0, keepdims=True)
    out_ref[1:2, :] += jnp.sum(e, axis=0, keepdims=True)


def final_kernel(blk_ref, x_ref, gn_ref, got_ref, gm_ref, g_ref, out_ref):
    n, rstd = row_norm(x_ref[...].astype(F32))
    f = (gn_ref[...] + got_ref[...]) * g_ref[...]
    out_ref[...] = (gm_ref[...] + row_norm_back(f, n, rstd)).astype(BF16)


def unpack_kernel(idx_ref, s_ref, out_ref):
    groups = out_ref.shape[0]
    part = s_ref.shape[1] // groups
    for g in range(groups):
        whole = jnp.concatenate(
            [s_ref[idx_ref[p], g * part : (g + 1) * part, :] for p in range(PIECES)], axis=0
        )
        out_ref[g] = whole.T


def unpack_rows_kernel(idx_ref, s_ref, out_ref):
    part = s_ref.shape[1]
    for p in range(PIECES):
        out_ref[p * part : (p + 1) * part, :] = s_ref[idx_ref[p]]


def unpack_att_kernel(ia_ref, ib_ref, a_ref, b_ref, qkv_ref, out_ref):
    part = a_ref.shape[1] // 2

    def whole(ref, i_ref, off):
        return jnp.concatenate(
            [ref[i_ref[p], off : off + part, :] for p in range(PIECES)], axis=0
        )

    qkv_ref[0] = whole(a_ref, ia_ref, 0).T
    qkv_ref[1] = whole(a_ref, ia_ref, part).T
    qkv_ref[2] = whole(b_ref, ib_ref, 0).T
    out_ref[...] = whole(b_ref, ib_ref, part)


def from_slot(a, k, size):
    return lax.ppermute(a, "mp", [(s, (s - k) % size) for s in range(size)])


def to_slot(a, k, size):
    return lax.ppermute(a, "mp", [(s, (s + k) % size) for s in range(size)])


def swap_plane(a, bit, size):
    return lax.ppermute(a, "dp", [(d, d ^ bit) for d in range(size)])


def storage_of(r, bits):
    return sum(jnp.where((r & bit) != 0, 1 << t, 0) for t, bit in enumerate(bits))


def offset_of(s, bits):
    return sum(bit for t, bit in enumerate(bits) if (s >> t) & 1)


class Stages:
    def __init__(self):
        self.live = {}
        self.flying = []

    def __setitem__(self, name, value):
        self.live[name] = value

    def __getitem__(self, name):
        return self.live[name]

    def pop(self, name):
        return self.live.pop(name)

    def fence(self, *still_flying):
        now = {n: a for n, a in self.live.items() if n not in still_flying}
        leaves, tree = jax.tree.flatten(now)
        self.live.update(jax.tree.unflatten(tree, lax.optimization_barrier(leaves)))


def shards(
    tokens,
    seg_ids,
    qkv_weight,
    qkv_bias,
    out_weight,
    out_bias,
    up_weight,
    up_bias,
    down_weight,
    down_bias,
    norm1_gain,
    norm1_shift,
    query_gain,
    query_shift,
    key_gain,
    norm2_gain,
    norm2_shift,
    cotangent,
):
    ndp = lax.axis_size("dp")
    nmp = lax.axis_size("mp")
    dp_no = lax.axis_index("dp")
    mp_no = lax.axis_index("mp")
    me = dp_no % PIECES
    row_count, width = tokens.shape
    share = row_count // nmp
    full = SEQ_LEN
    assert full == 2 * share and nmp == 4 and ndp % PIECES == 0
    e = qkv_weight.shape[2]
    part = e // PIECES
    units = up_weight.shape[1]
    upart = units // PIECES
    half = PIECES // 2
    core, px, py = 1, 2, 4

    vmem = pl.BlockSpec(memory_space=pltpu.VMEM)
    smem = pl.BlockSpec(memory_space=pltpu.SMEM)
    row1 = lambda v: v.reshape(1, -1)
    col = lambda v: v.reshape(-1, 1)
    swap = lambda a, bit: swap_plane(a, bit, ndp)
    get = lambda a, k: from_slot(a, k, nmp)
    put = lambda a, k: to_slot(a, k, nmp)
    v = Stages()

    qkv_t = jnp.swapaxes(qkv_weight, 1, 2).reshape(3, PIECES, part, width)
    out_p = out_weight.reshape(PIECES, part, width)
    att_a0 = jnp.concatenate([qkv_t[0], qkv_t[1]], axis=1).astype(F32)
    att_b0 = jnp.concatenate([qkv_t[2], out_p], axis=1).astype(F32)
    up_t = up_weight.T.reshape(PIECES, upart, width)
    down_p = down_weight.reshape(PIECES, upart, width)

    def pick(a, r):
        return lax.dynamic_index_in_dim(a, me ^ r, 0, keepdims=False)

    att_piece = jnp.concatenate([pick(att_a0, 0), pick(att_b0, 0)], axis=0)
    mlp_piece = jnp.concatenate([pick(up_t, 0), pick(down_p, 0)], axis=0).astype(F32)
    up_half = [
        jnp.stack([pick(up_t, offset_of(s, BITS_A)) for s in h]) for h in (range(4), range(4, 8))
    ]
    down_half = [
        jnp.stack([pick(down_p, offset_of(s, BITS_B)) for s in h])
        for h in (range(4), range(4, 8))
    ]
    ub = up_bias.reshape(PIECES, 1, upart)
    ub0 = jnp.stack([pick(ub, offset_of(s, BITS_A)) for s in range(PIECES)])
    bias_pack = jnp.concatenate([qkv_bias.reshape(-1), ub0.reshape(-1)])

    numbers = jnp.arange(PIECES, dtype=jnp.int32)
    idx_a = storage_of(numbers ^ me, BITS_A).astype(jnp.int32)
    idx_b = storage_of(numbers ^ me, BITS_B).astype(jnp.int32)

    block = 256
    per = share // block
    steps = 2 * per
    tile_no = jnp.arange(steps, dtype=jnp.int32)
    blk = jnp.where(tile_no < per, mp_no * per + tile_no, (mp_no ^ 1) * per + tile_no - per).astype(
        jnp.int32
    )
    const2 = lambda t, b: (0, 0)
    tok_spec = pl.BlockSpec((block, width), lambda t, b: (b[t], 0))
    run_spec = pl.BlockSpec((block, width), lambda t, b: (t, 0))
    vec_spec = pl.BlockSpec((1, width), const2)

    def run_norm1():
        return call(
            norm1_kernel,
            sds((full, width), BF16),
            flops=full * width * 10,
            bytes_accessed=full * width * 4,
            grid_spec=pltpu.PrefetchScalarGridSpec(
                num_scalar_prefetch=1,
                grid=(steps,),
                in_specs=[tok_spec, vec_spec, vec_spec],
                out_specs=run_spec,
            ),
        )(blk, tokens, row1(norm1_gain), row1(norm1_shift))

    seg_own = lax.dynamic_slice_in_dim(seg_ids, mp_no * share, share, 0)
    seg_other = lax.dynamic_slice_in_dim(seg_ids, (mp_no ^ 1) * share, share, 0)
    seg_keys = jnp.concatenate([seg_own, seg_other])
    qhot = (
        lax.broadcasted_iota(jnp.int32, (SEG_COLS, share), 0) == seg_own[None, :]
    ).astype(BF16)
    kmask = jnp.where(
        lax.broadcasted_iota(jnp.int32, (full, SEG_COLS), 1) == seg_keys[:, None], 0.0, -1e30
    ).astype(BF16)
    qg, qs, kg = col(query_gain), col(query_shift), col(key_gain)

    def run_attn_fwd(k, at, wa, wb, ia, ib, bias):
        names = ("qpre", "kpre", "vt", "wt", "ow", "mixt", "mixf", "l")
        outs = call(
            functools.partial(attn_fwd_kernel, at),
            (
                sds((e, share), F32),
                sds((e, full), F32),
                sds((e, full), BF16),
                sds((3 * e, width), BF16),
                sds((e, width), BF16),
                sds((e, share), BF16),
                sds((e, share), F32),
                sds((8, share), F32),
            ),
            flops=2 * (full * width * e * 5 // 2 + full * share * e * 8),
            bytes_accessed=8_000_000,
            in_specs=[smem, smem] + [vmem] * 9,
            out_specs=(vmem,) * 8,
            scratch_shapes=[
                pltpu.VMEM((2 * DH + SEG_COLS, share), BF16),
                pltpu.VMEM((full, 2 * DH + SEG_COLS), BF16),
            ],
        )(
            ia,
            ib,
            v["normed"],
            wa,
            wb,
            bias[: 3 * e].reshape(3 * e, 1),
            qg,
            qs,
            kg,
            kmask,
            qhot,
        )
        v[f"st{k}"] = dict(zip(names, outs))

    def run_out():
        own_spec = pl.BlockSpec((share, width), lambda t, b: (b[0] // per, 0))
        whole = lambda shape: pl.BlockSpec(shape, lambda t, b: (0,) * len(shape))
        v["middle"], v["second"] = call(
            functools.partial(out_norm2_kernel, nmp),
            (sds((share, width), F32), sds((share, width), BF16)),
            flops=2 * share * width * e * nmp,
            bytes_accessed=8_000_000,
            grid_spec=pltpu.PrefetchScalarGridSpec(
                num_scalar_prefetch=1,
                grid=(1,),
                in_specs=[own_spec]
                + [whole((e, share))] * nmp
                + [whole((e, width))] * nmp
                + [whole((1, width))] * 3,
                out_specs=(whole((share, width)), whole((share, width))),
            ),
        )(
            blk,
            tokens,
            *[v[f"st{k}"]["mixt"] for k in range(nmp)],
            *[v[f"st{k}"]["ow"] for k in range(nmp)],
            row1(out_bias),
            row1(norm2_gain),
            row1(norm2_shift),
        )

    piece_spec = pl.BlockSpec((1, upart, width), lambda t: (t, 0, 0))
    swap_spec = pl.BlockSpec((1, upart, width), lambda t: ((t % 2) * 2 + t // 2, 0, 0))
    bias_spec = pl.BlockSpec((1, 1, upart), lambda t: (t, 0, 0))
    rows_spec = pl.BlockSpec((share, width), lambda t: (0, 0))

    def run_mlp(k, up, down, bias, first):
        ubk = bias[3 * e :].reshape(PIECES, 1, upart)
        args = [
            v["second"], v["cot"], up[0], up[1], ubk[:half], ubk[half:], down[0], down[1],
        ]
        specs = [
            rows_spec, rows_spec, piece_spec, piece_spec, bias_spec, bias_spec, swap_spec, swap_spec,
        ]
        alias = {}
        if not first:
            args += [v["acc"], v["gs"]]
            specs += [rows_spec, rows_spec]
            alias = {8: 0, 9: 1}
        res = call(
            functools.partial(mlp_kernel, first),
            (
                sds((share, width), F32),
                sds((share, width), F32),
                *[sds((half, upart, width), F32)] * 4,
                *[sds((half, 1, upart), F32)] * 2,
            ),
            flops=2 * share * width * units * 6,
            bytes_accessed=16_000_000,
            grid=(half,),
            in_specs=specs,
            out_specs=(
                rows_spec,
                rows_spec,
                piece_spec,
                piece_spec,
                swap_spec,
                swap_spec,
                bias_spec,
                bias_spec,
            ),
            input_output_aliases=alias,
        )(*args)
        v["acc"], v["gs"] = res[0], res[1]
        v[f"u{k}"] = (res[2], res[3])
        v[f"d{k}"] = (res[4], res[5])
        v[f"ubg{k}"] = jnp.concatenate([res[6], res[7]], axis=0)[:, 0, :]

    def run_mid():
        *gmts, bo, gm, keep, send, mst = call(
            functools.partial(mid_kernel, nmp),
            (
                *[sds((e, share), BF16)] * nmp,
                sds((share, width), BF16),
                sds((share, width), F32),
                sds((half, nmp * part, width), F32),
                sds((half, nmp * part, width), F32),
                sds((8, width), F32),
            ),
            flops=2 * share * width * e * nmp * 2,
            bytes_accessed=12_000_000,
            in_specs=[smem] + [vmem] * (6 + 2 * nmp),
            out_specs=(vmem,) * (5 + nmp),
        )(
            idx_a,
            v["middle"],
            v.pop("acc"),
            v.pop("gs"),
            v["cot"],
            row1(down_bias),
            row1(norm2_gain),
            *[v[f"st{k}"]["ow"] for k in range(nmp)],
            *[v[f"st{k}"]["mixt"] for k in range(nmp)],
        )
        v["block_out"], v["gm"], v["mst"] = bo, gm, mst
        for k in range(nmp):
            v[f"gmt{k}"] = gmts[k]
        v["o"] = (keep, send)

    def run_attn_bwd(k, idx, first):
        st = v.pop(f"st{k}")
        args = [
            idx, v["normed"], st["qpre"], st["kpre"], st["vt"], st["wt"], v.pop(f"gmt{k}"), st["mixf"],
            st["l"], qg, qs, kg, kmask, qhot,
        ]
        specs = [smem] + [vmem] * 13
        alias = {}
        if not first:
            args.append(v["gn"])
            specs.append(vmem)
            alias = {len(args) - 1: 2}
        keep, send, gn, hst, gb = call(
            functools.partial(attn_bwd_kernel, first),
            (
                sds((half, 3 * part, width), F32),
                sds((half, 3 * part, width), F32),
                sds((full, width), F32),
                sds((3, DH, 128), F32),
                sds((3 * e, 128), F32),
            ),
            flops=2 * (full * width * e * 5 + full * share * e * 20),
            bytes_accessed=14_000_000,
            in_specs=specs,
            out_specs=(vmem,) * 5,
            scratch_shapes=[
                pltpu.VMEM((2 * DH + SEG_COLS, share), BF16),
                pltpu.VMEM((full, 2 * DH + SEG_COLS), BF16),
                pltpu.VMEM((3 * e, full), BF16),
            ],
            input_output_aliases=alias,
        )(*args)
        v[f"q{k}"] = (keep, send)
        v["gn"] = gn
        v[f"hst{k}"] = hst
        v[f"qbg{k}"] = jnp.sum(gb, axis=1)

    def g1(n):
        a, b = v[n + "a"], v[n + "b"]
        v[n + "a"] = (a, swap(a, px))
        v[n + "b"] = (b, swap(b, py))

    def g2(n):
        a, b = (jnp.stack(v[n + t]) for t in "ab")
        v[n + "a"] = (a, swap(a, py))
        v[n + "b"] = (b, swap(b, px))

    def g3(n):
        a, b = (jnp.concatenate(v[n + t], axis=0) for t in "ab")
        v[n + "a"] = (a, swap(a, core))
        v[n + "b"] = (b, swap(b, core))

    def r1(n):
        keep, send = v[n]
        v[n] = (keep, swap(send, core))

    def r2(n, kind):
        keep, got = v[n]
        keep_sum = keep[:2] + got[:2]
        v[n] = (keep_sum, swap(keep[2:] + got[2:], py if kind == "a" else px))

    def r3(n, kind):
        keep, got = v[n]
        v[n] = (keep[0] + got[0], swap(keep[1] + got[1], px if kind == "a" else py))

    def r4(n):
        keep, got = v[n]
        v[n] = keep + got

    v["cot"] = lax.dynamic_slice_in_dim(cotangent, mp_no * share, share, 0)
    v["att_piece"], v["mlp_piece"], v["bias"] = att_piece, mlp_piece, bias_pack
    v["t1"] = get(att_piece, 1)
    v["t3"] = get(att_piece, 3)
    for k in range(1, nmp):
        v[f"bias{k}"] = get(bias_pack, k)
    v["normed"] = run_norm1()
    run_attn_fwd(0, 0, att_a0[:, None], att_b0[:, None], numbers, numbers, bias_pack)
    v.fence()
    hp = 2 * part
    t1, t3 = v.pop("t1"), v.pop("t3")
    v["ta"] = jnp.stack([t1[:hp], t3[:hp]])
    v["tb"] = jnp.stack([t1[hp:], t3[hp:]])
    g1("t")
    v["t2"] = get(v["att_piece"], 2)
    v.fence()
    g2("t")
    v["m1"] = get(v["mlp_piece"], 1)
    v.fence()
    g3("t")
    t2 = v.pop("t2")
    v["sa"], v["sb"] = t2[:hp][None], t2[hp:][None]
    g1("s")
    m1 = v.pop("m1")
    v["m1a"], v["m1b"] = m1[:upart], m1[upart:]
    g1("m1")
    v["m3"] = get(v["mlp_piece"], 3)
    v.fence()
    wa, wb = (jnp.concatenate(v.pop("t" + t), axis=0) for t in "ab")
    wa, wb = (w.reshape(PIECES, 2, hp, width) for w in (wa, wb))
    v["wa"], v["wb"] = wa, wb
    run_attn_fwd(1, 0, wa, wb, idx_a, idx_b, v["bias1"])
    g2("s")
    g2("m1")
    v["m2"] = get(v["mlp_piece"], 2)
    v.fence("m2")
    run_attn_fwd(3, 1, v.pop("wa"), v.pop("wb"), idx_a, idx_b, v["bias3"])
    g3("s")
    g3("m1")
    m3 = v.pop("m3")
    v["m3a"], v["m3b"] = m3[:upart], m3[upart:]
    g1("m3")
    v.fence()
    wa, wb = (jnp.concatenate(v.pop("s" + t), axis=0) for t in "ab")
    wa, wb = (w.reshape(PIECES, 1, hp, width) for w in (wa, wb))
    run_attn_fwd(2, 0, wa, wb, idx_a, idx_b, v["bias2"])
    run_out()
    g2("m3")
    m2 = v.pop("m2")
    v["m2a"], v["m2b"] = m2[:upart], m2[upart:]
    g1("m2")
    v.fence()
    run_mlp(0, up_half, down_half, v["bias"], True)
    g3("m3")
    g2("m2")
    v.fence()
    run_mlp(1, v.pop("m1a"), v.pop("m1b"), v["bias1"], False)
    g3("m2")
    r1("u0")
    r1("d0")
    v.fence()
    run_mlp(3, v.pop("m3a"), v.pop("m3b"), v["bias3"], False)
    r2("u0", "a")
    r2("d0", "b")
    r1("u1")
    r1("d1")
    v.fence()
    run_mlp(2, v.pop("m2a"), v.pop("m2b"), v["bias2"], False)
    r3("u0", "a")
    r3("d0", "b")
    r2("u1", "a")
    r2("d1", "b")
    r1("u3")
    r1("d3")
    v.fence()
    run_mid()
    r4("u0")
    r4("d0")
    r3("u1", "a")
    r3("d1", "b")
    r2("u3", "a")
    r2("d3", "b")
    r1("u2")
    r1("d2")
    v.fence()

    def join(k):
        r4(f"u{k}")
        r4(f"d{k}")
        return jnp.concatenate([v.pop(f"u{k}"), v.pop(f"d{k}")], axis=0)

    run_attn_bwd(1, idx_b, True)
    r3("u3", "a")
    r3("d3", "b")
    r2("u2", "a")
    r2("d2", "b")
    v["z1"] = put(join(1), 1)
    r1("o")
    v.fence()
    run_attn_bwd(2, idx_b, False)
    r3("u2", "a")
    r3("d2", "b")
    v["z3"] = put(join(3), 3)
    r2("o", "a")
    r1("q1")
    v.fence()
    run_attn_bwd(3, idx_a, False)
    v["z2"] = put(join(2), 2)
    r3("o", "a")
    r2("q1", "b")
    r1("q2")
    v.fence()

    def high_bits(a):
        bit = PIECES
        while bit < ndp:
            a = a + swap(a, bit)
            bit *= 2
        return a

    run_attn_bwd(0, idx_b, False)
    mlp_sum = jnp.concatenate([v.pop("u0"), v.pop("d0")], axis=0)
    mlp_sum = high_bits(mlp_sum + v.pop("z1") + v.pop("z2") + v.pop("z3"))
    v["ma"], v["mb"] = mlp_sum[:upart], mlp_sum[upart:]
    g1("m")
    r4("o")
    r3("q1", "b")
    r2("q2", "b")
    r1("q3")
    v.fence()
    n1_stats = call(
        norm1_stats_kernel,
        sds((8, width), F32),
        flops=full * width * 10,
        bytes_accessed=full * width * 6,
        grid_spec=pltpu.PrefetchScalarGridSpec(
            num_scalar_prefetch=1,
            grid=(steps,),
            in_specs=[tok_spec, run_spec],
            out_specs=pl.BlockSpec((8, width), const2),
        ),
    )(blk, tokens, v["gn"])
    v["got"] = lax.ppermute(v["gn"][share:], "mp", [(s, s ^ 1) for s in range(nmp)])
    r1("q0")
    g2("m")
    r4("q1")
    r3("q2", "b")
    r2("q3", "a")
    head_sum = jnp.sum(sum(v.pop(f"hst{k}") for k in range(nmp)), axis=-1)
    copied = jnp.concatenate(
        [v.pop("mst")[:4].reshape(-1), n1_stats[:2].reshape(-1), head_sum.reshape(-1)]
    )
    own_parts = [
        jnp.concatenate([v.pop(f"qbg{k}"), jnp.take(v.pop(f"ubg{k}"), idx_a, axis=0).reshape(-1)])
        for k in range(nmp)
    ]
    nc = copied.shape[0]
    no = own_parts[0].shape[0]
    v["small"] = jnp.concatenate([copied] + own_parts)
    v.fence("got")
    o = v.pop("o")
    v["o"] = o

    def joined(k):
        return jnp.concatenate([v.pop(f"q{k}"), v["o"][k * part : (k + 1) * part]], axis=0)

    r2("q0", "b")
    v["small"] = v["small"] + swap(v["small"], core)
    r4("q2")
    r3("q3", "a")
    g3("m")
    v["y1"] = put(joined(1), 1)
    v["y2"] = put(joined(2), 2)
    v.fence("got", "y1", "y2")
    r3("q0", "b")
    v["small"] = v["small"] + swap(v["small"], px)
    r4("q3")
    v["y3"] = put(joined(3), 3)
    v.fence("got", "y1", "y2", "y3")

    def unpack(kernel, state, idx, shape):
        return call(
            kernel,
            sds(shape, F32),
            bytes_accessed=2 * 4 * math.prod(shape),
            in_specs=[smem, vmem],
            out_specs=vmem,
        )(idx, state)

    r4("q0")
    v["small"] = v["small"] + swap(v["small"], py)
    v["up_g"] = unpack(
        unpack_kernel, jnp.concatenate(v.pop("ma"), axis=0), idx_a, (1, width, units)
    )[0]
    v["down_g"] = unpack(
        unpack_rows_kernel, jnp.concatenate(v.pop("mb"), axis=0), idx_b, (units, width)
    )
    v.fence()
    att_sum = high_bits(joined(0) + v.pop("y1") + v.pop("y2") + v.pop("y3"))
    v["wa"], v["wb"] = att_sum[:hp], att_sum[hp:]
    g1("w")
    small = high_bits(v.pop("small"))
    small_sum = small[: nc + no]
    for k in range(1, nmp):
        sent = jnp.concatenate([small[:nc], small[nc + k * no : nc + (k + 1) * no]])
        small_sum = small_sum + put(sent, k)
    v["input_grad"] = call(
        final_kernel,
        sds((share, width), BF16),
        flops=share * width * 20,
        bytes_accessed=share * width * 16,
        grid_spec=pltpu.PrefetchScalarGridSpec(
            num_scalar_prefetch=1,
            grid=(per,),
            in_specs=[tok_spec, run_spec, run_spec, run_spec, vec_spec],
            out_specs=run_spec,
        ),
    )(blk, tokens, v["gn"], v["got"], v["gm"], row1(norm1_gain))
    v.fence()
    g2("w")
    v.fence()
    g3("w")
    wa, wb = (jnp.concatenate(v.pop("w" + t), axis=0) for t in "ab")
    qkv_weight_grad, out_weight_grad = call(
        unpack_att_kernel,
        (sds((3, width, e), F32), sds((e, width), F32)),
        bytes_accessed=2 * 4 * 4 * width * e,
        in_specs=[smem, smem, vmem, vmem],
        out_specs=(vmem, vmem),
    )(idx_a, idx_b, wa, wb)

    rows_of = small_sum[: 6 * width].reshape(6, width)
    heads_of = small_sum[6 * width : nc].reshape(3, DH)
    qkv_bias_grad = small_sum[nc : nc + 3 * e].reshape(3, e)
    up_bias_grad = small_sum[nc + 3 * e :]
    return (
        v["block_out"],
        v["input_grad"],
        qkv_weight_grad,
        qkv_bias_grad,
        out_weight_grad,
        rows_of[2],
        v["up_g"],
        up_bias_grad,
        v["down_g"],
        rows_of[3],
        rows_of[4],
        rows_of[5],
        heads_of[0],
        heads_of[1],
        heads_of[2],
        rows_of[0],
        rows_of[1],
    )


def solution(mesh):
    in_specs = (
        P("dp", None),
        P("dp"),
        P(None, None, "mp"),
        P(None, "mp"),
        P("mp", None),
        P(),
        P(None, "mp"),
        P("mp"),
        P("mp", None),
        P(),
        P(),
        P(),
        P(),
        P(),
        P(),
        P(),
        P(),
        P("dp", None),
    )
    out_specs = (
        P(("dp", "mp"), None),
        P(("dp", "mp"), None),
        P(None, None, "mp"),
        P(None, "mp"),
        P("mp", None),
        P(),
        P(None, "mp"),
        P("mp"),
        P("mp", None),
        P(),
        P(),
        P(),
        P(),
        P(),
        P(),
        P(),
        P(),
    )
    return jax.shard_map(shards, mesh=mesh, in_specs=in_specs, out_specs=out_specs, check_vma=False)
```

time: 722 us -> 523 us (0.72)
  waiting for transfers between devices: 311 us -> 126 us
  starting transfers between devices: 124 us -> 90.9 us
  other arithmetic: 57.4 us -> 69.2 us
    ppermute x81 -> x84, waiting for transfers between devices: 243 us -> 95 us  [swap_plane(): return lax.ppermute(a, 'dp', [(d, d ^ bit) for d in range(size)])]
    add x31 -> x45, other arithmetic: 6.48 us -> 38.8 us  [the longest x13 21.5 us: r2(): v[n] = (keep_sum, swap(keep[2:] + got[2:], py if kind == 'a' else px))]
    ppermute x15 -> x9, starting transfers between devices: 40 us -> 14.4 us  [to_slot(): return lax.ppermute(a, 'mp', [(s, (s + k) % size) for s in range(size)])]
    ppermute x12 -> x9, waiting for transfers between devices: 36.1 us -> 13.1 us  [from_slot(): return lax.ppermute(a, 'mp', [(s, (s - k) % size) for s in range(size)])]
    concatenate x37 -> x19, other arithmetic: 35.3 us -> 15.5 us  [the longest x4 2.83 us: run_mlp(): v[f'ubg{k}'] = jnp.concatenate([res[6], res[7]], axis=0)[:, 0, :]]
    ppermute x15 -> x9, waiting for transfers between devices: 31.6 us -> 18 us  [to_slot(): return lax.ppermute(a, 'mp', [(s, (s + k) % size) for s in range(size)])]
    ppermute x1, starting transfers between devices: 8.4 us -> 0.07 us  [shards(): lax.ppermute(v['gn'][share:], 'mp', [(s, s ^ 1) for s in range(nmp)])]
    concatenate x1 -> x15, local copies, waits for them, and re-layouts: 0.08 us -> 8.31 us  [the longest x12 8.03 us: g3(): a, b = (jnp.concatenate(v[n + t], axis=0) for t in 'ab')]
  transfers between devices with their start and end apart: 109 -> 103, of which waited for: 39 -> 35; matrix products, arithmetic and copies ran while one was open for 12% -> 18% of each run, Pallas kernels for 19% -> 32%
where the time goes in v2:
time: 523 us; the launch traced here: 516 us
  Pallas kernels  171 us (33%)
  waiting for transfers between devices  126 us (24%)
  starting transfers between devices  90.9 us (17%)
  other arithmetic  69.2 us (13%)
  local copies, waits for them, and re-layouts  56.5 us (11%)
    ppermute x84, waiting for transfers between devices, swap_plane(): return lax.ppermute(a, 'dp', [(d, d ^ bit) for d in range(size)])  95 us
    ppermute x84, starting transfers between devices, swap_plane(): return lax.ppermute(a, 'dp', [(d, d ^ bit) for d in range(size)])  63.1 us
    pallas_call x4, Pallas kernels, run_attn_bwd(): call(functools.partial(attn_bwd_kernel, first), (sds((half, 3 * part, wid...  54.1 us
    pallas_call x4, Pallas kernels, run_mlp(): call(functools.partial(mlp_kernel, first), (sds((share, width), F32), sds...  49.7 us
    pallas_call x4, Pallas kernels, run_attn_fwd(): call(functools.partial(attn_fwd_kernel, at), (sds((e, share), F32), sds((...  26.7 us
    add x13, other arithmetic, r2(): v[n] = (keep_sum, swap(keep[2:] + got[2:], py if kind == 'a' else px))  21.5 us
    ppermute x9, waiting for transfers between devices, to_slot(): return lax.ppermute(a, 'mp', [(s, (s + k) % size) for s in range(size)])  18 us
    unnamed x178, local copies, waits for them, and re-layouts  16.9 us
  transfers between devices with their start and end apart: 103, of which 35 were waited for; matrix products, arithmetic and copies ran while one was open for 18% of the time, Pallas kernels for 32%

profile of v2, /device:TPU:0, one launch (start us, length us, event | category | flops | bytes accessed | tf_op | source)
XLA Modules:
  0.0 516.5 jit_solution(18029611203818841127)
XLA Ops:
  3.9 5.0 collective-permute-start
  25.4 5.0 shard_map.305.x_ref
  32.5 6.4 %shard_map.306 = (f32[192,512]{1,0:T(8,128)}, f32[192,1024]{1,0:T(8,128)}, bf16[192,1024]{1,0:T(8,128)(2,1)}, bf16[576,768]{1,0:T(8,128)(2,1)}, bf16[192,768]{1,...) custom-call(s32[8]{0:T(128)} %iota.28.ia_ref.ib_ref, s32[8]{0:T(128)} %iota.28.ia_ref.ib_ref, ...), custom_call_target="tpu_custom_call" | custom-call | flops 2365587456 | bytes 8000000 | tf_op jit(solution)/shard_map/pallas_call | solution.py:535
  51.5 8.6 %collective-permute-done.5 = f32[96,768]{1,0:T(8,128)S(1)} collective-permute-done((f32[96,768]{1,0:T(8,128)}, f32[96,768]{1,0:T(8,128)S(1)}, u32[]{:S(2)}, u32[]{:S(2)}) %collective-permute-start.5) | collective-permute-done | bytes 294944 | tf_op jit(solution)/shard_map/ppermute | solution.py:385
  63.2 11.4 %collective-permute-done.10 = f32[2,2,48,768]{3,2,1,0:T(8,128)S(1)} collective-permute-done((f32[2,2,48,768]{3,2,1,0:T(8,128)S(1)}, f32[2,2,48,768]{3,2,1,0:T(8,128)S(1)}, u32[]{:S(2)}, u32[]{:S(2)}) %collective-permute-start.10) | collective-permute-done | bytes 589856 | tf_op jit(solution)/shard_map/ppermute | solution.py:393
  86.2 4.6 collective-permute-done.11
  105.2 7.0 %shard_map.307 = (f32[192,512]{1,0:T(8,128)}, f32[192,1024]{1,0:T(8,128)}, bf16[192,1024]{1,0:T(8,128)(2,1)}, bf16[576,768]{1,0:T(8,128)(2,1)}, bf16[192,768]{1,...) custom-call(s32[8]{0:T(128)} %get-tuple-element.1819.ia_ref.idx_ref, ...), custom_call_target="tpu_custom_call" | custom-call | flops 2365587456 | bytes 8000000 | tf_op jit(solution)/shard_map/pallas_call | solution.py:535
  112.3 5.3 %collective-permute-done.19 = f32[2,96,768]{2,1,0:T(8,128)} collective-permute-done((f32[2,96,768]{2,1,0:T(8,128)S(1)}, f32[2,96,768]{2,1,0:T(8,128)}, u32[]{:S(2)}, u32[]{:S(2)}) %collective-permute-start.19) | collective-permute-done | bytes 589856 | tf_op jit(solution)/shard_map/ppermute | solution.py:393
  129.7 4.1 collective-permute-done.25
  137.1 7.0 %shard_map.308 = (f32[192,512]{1,0:T(8,128)}, f32[192,1024]{1,0:T(8,128)}, bf16[192,1024]{1,0:T(8,128)(2,1)}, bf16[576,768]{1,0:T(8,128)(2,1)}, bf16[192,768]{1,...) custom-call(s32[8]{0:T(128)} %get-tuple-element.1819.ia_ref.idx_ref, ...), custom_call_target="tpu_custom_call" | custom-call | flops 2365587456 | bytes 8000000 | tf_op jit(solution)/shard_map/pallas_call | solution.py:535
  152.7 6.3 %shard_map.309 = (f32[192,512]{1,0:T(8,128)}, f32[192,1024]{1,0:T(8,128)}, bf16[192,1024]{1,0:T(8,128)(2,1)}, bf16[576,768]{1,0:T(8,128)(2,1)}, bf16[192,768]{1,...) custom-call(s32[8]{0:T(128)} %get-tuple-element.1819.ia_ref.idx_ref, ...), custom_call_target="tpu_custom_call" | custom-call | flops 2365587456 | bytes 8000000 | tf_op jit(solution)/shard_map/pallas_call | solution.py:535
  159.0 5.0 shard_map.310
  175.1 11.4 %shard_map.311 = (f32[512,768]{1,0:T(8,128)}, f32[512,768]{1,0:T(8,128)}, f32[4,96,768]{2,1,0:T(8,128)}, f32[4,96,768]{2,1,0:T(8,128)}, f32[4,96,768]{2,1,0:T(8,...) custom-call(bf16[512,768]{1,0:T(8,128)(2,1)} %get-tuple-element.1240.refs_0_, ...), custom_call_target="tpu_custom_call" | custom-call | flops 3623878656 | bytes 16000000 | tf_op jit(solution)/shard_map/pallas_call | solution.py:615
  193.0 12.7 %shard_map.312 = (f32[512,768]{1,0:T(8,128)}, f32[512,768]{1,0:T(8,128)}, f32[4,96,768]{2,1,0:T(8,128)}, f32[4,96,768]{2,1,0:T(8,128)}, f32[4,96,768]{2,1,0:T(8,...) custom-call(bf16[512,768]{1,0:T(8,128)(2,1)} %get-tuple-element.1240, ...), custom_call_target="tpu_custom_call", output_to_operand_aliasing={{0}: (8, {}), {1}: (9, {})} | custom-call | flops 3623878656 | bytes 16000000 | tf_op jit(solution)/shard_map/pallas_call | solution.py:615
  213.4 12.7 %shard_map.313 = (f32[512,768]{1,0:T(8,128)}, f32[512,768]{1,0:T(8,128)}, f32[4,96,768]{2,1,0:T(8,128)}, f32[4,96,768]{2,1,0:T(8,128)}, f32[4,96,768]{2,1,0:T(8,...) custom-call(bf16[512,768]{1,0:T(8,128)(2,1)} %get-tuple-element.1240, ...), custom_call_target="tpu_custom_call", output_to_operand_aliasing={{0}: (8, {}), {1}: (9, {})} | custom-call | flops 3623878656 | bytes 16000000 | tf_op jit(solution)/shard_map/pallas_call | solution.py:615
  237.4 5.6 %collective-permute-done.48 = f32[96,768]{1,0:T(8,128)S(1)} collective-permute-done((f32[96,768]{1,0:T(8,128)S(1)}, f32[96,768]{1,0:T(8,128)S(1)}, u32[]{:S(2)}, u32[]{:S(2)}) %collective-permute-start.48) | collective-permute-done | bytes 294944 | tf_op jit(solution)/shard_map/ppermute | solution.py:393
  243.6 13.0 %shard_map.314 = (f32[512,768]{1,0:T(8,128)}, f32[512,768]{1,0:T(8,128)}, f32[4,96,768]{2,1,0:T(8,128)}, f32[4,96,768]{2,1,0:T(8,128)}, f32[4,96,768]{2,1,0:T(8,...) custom-call(bf16[512,768]{1,0:T(8,128)(2,1)} %get-tuple-element.1240, ...), custom_call_target="tpu_custom_call", output_to_operand_aliasing={{0}: (8, {}), {1}: (9, {})} | custom-call | flops 3623878656 | bytes 16000000 | tf_op jit(solution)/shard_map/pallas_call | solution.py:615
  265.6 6.8 %collective-permute-done.54 = f32[96,768]{1,0:T(8,128)S(1)} collective-permute-done((f32[96,768]{1,0:T(8,128)S(1)}, f32[96,768]{1,0:T(8,128)S(1)}, u32[]{:S(2)}, u32[]{:S(2)}) %collective-permute-start.54) | collective-permute-done | bytes 294944 | tf_op jit(solution)/shard_map/ppermute | solution.py:393
  273.1 9.6 %shard_map.315 = (bf16[192,512]{1,0:T(8,128)(2,1)}, bf16[192,512]{1,0:T(8,128)(2,1)}, bf16[192,512]{1,0:T(8,128)(2,1)}, bf16[192,512]{1,0:T(8,128)(2,1)}, bf16[5...) custom-call(s32[8]{0:T(128)} %get-tuple-element.1819.ia_ref.idx_ref,, ...), custom_call_target="tpu_custom_call" | custom-call | flops 1207959552 | bytes 12000000 | tf_op jit(solution)/shard_map/pallas_call | solution.py:645
  295.3 12.7 %shard_map.316 = (f32[4,72,768]{2,1,0:T(8,128)}, f32[4,72,768]{2,1,0:T(8,128)}, f32[1024,768]{1,0:T(8,128)}, f32[3,64,128]{2,1,0:T(8,128)}, f32[576,128]{1,0:T(8,128)}) custom-call(s32[8]{0:T(128)} %get-tuple-element.1820.ib_ref.idx_ref, bf16[1024,768]{1,0:T(8,128)(2,1)} %shard_map.305.x_ref, f32[192,512]{1,0:T(8,128)} %get-tuple-element.1383.qpre_ref, ...), custom_call_target="tpu_custom_call" | custom-call | flops 5536481280 | bytes 14000000 | tf_op jit(solution)/shard_map/pallas_call | solution.py:687
  325.9 13.8 %shard_map.317 = (f32[4,72,768]{2,1,0:T(8,128)}, f32[4,72,768]{2,1,0:T(8,128)}, f32[1024,768]{1,0:T(8,128)}, f32[3,64,128]{2,1,0:T(8,128)}, f32[576,128]{1,0:T(8,128)}) custom-call(s32[8]{0:T(128)} %get-tuple-element.1820.ib_ref.idx_ref, bf16[1024,768]{1,0:T(8,128)(2,1)} %shard_map.305.x_ref, ...), custom_call_target="tpu_custom_call", output_to_operand_aliasing={{2}: (14, {})} | custom-call | flops 5536481280 | bytes 14000000 | tf_op jit(solution)/shard_map/pallas_call | solution.py:687
  350.1 13.8 %shard_map.318 = (f32[4,72,768]{2,1,0:T(8,128)}, f32[4,72,768]{2,1,0:T(8,128)}, f32[1024,768]{1,0:T(8,128)}, f32[3,64,128]{2,1,0:T(8,128)}, f32[576,128]{1,0:T(8,128)}) custom-call(s32[8]{0:T(128)} %get-tuple-element.1819.ia_ref.idx_ref, bf16[1024,768]{1,0:T(8,128)(2,1)} %shard_map.305.x_ref, ...), custom_call_target="tpu_custom_call", output_to_operand_aliasing={{2}: (14, {})} | custom-call | flops 5536481280 | bytes 14000000 | tf_op jit(solution)/shard_map/pallas_call | solution.py:687
  366.5 5.4 %collective-permute-done.71 = f32[192,768]{1,0:T(8,128)} collective-permute-done((f32[192,768]{1,0:T(8,128)}, f32[192,768]{1,0:T(8,128)}, u32[]{:S(2)}, u32[]{:S(2)}) %collective-permute-start.71) | collective-permute-done | bytes 589856 | tf_op jit(solution)/shard_map/ppermute | solution.py:389
  380.8 13.9 %shard_map.319 = (f32[4,72,768]{2,1,0:T(8,128)}, f32[4,72,768]{2,1,0:T(8,128)}, f32[1024,768]{1,0:T(8,128)}, f32[3,64,128]{2,1,0:T(8,128)}, f32[576,128]{1,0:T(8,128)}) custom-call(s32[8]{0:T(128)} %get-tuple-element.1820.ib_ref.idx_ref, bf16[1024,768]{1,0:T(8,128)(2,1)} %shard_map.305.x_ref, ...), custom_call_target="tpu_custom_call", output_to_operand_aliasing={{2}: (14, {})} | custom-call | flops 5536481280 | bytes 14000000 | tf_op jit(solution)/shard_map/pallas_call | solution.py:687
  406.2 5.5 %shard_map.320 = f32[8,768]{1,0:T(8,128)} custom-call(s32[4]{0:T(128)} %compare_select_fusion.1.blk_ref, bf16[2048,768]{1,0:T(8,128)(2,1)} %x_ref.7, f32[1024,768]{1,0:T(8,128)} %get-tuple-element.1639.gn_ref), custom_call_target="tpu_custom_call" | custom-call | flops 7864320 | bytes 4718592 | tf_op jit(solution)/shard_map/pallas_call | solution.py:874
  414.3 14.3 %collective-permute-done.80 = f32[72,768]{1,0:T(8,128)S(1)} collective-permute-done((f32[72,768]{1,0:T(8,128)}, f32[72,768]{1,0:T(8,128)S(1)}, u32[]{:S(2)}, u32[]{:S(2)}) %collective-permute-start.80) | collective-permute-done | bytes 221216 | tf_op jit(solution)/shard_map/ppermute | solution.py:393
  437.0 13.8 %collective-permute-done.85 = f32[72,768]{1,0:T(8,128)S(1)} collective-permute-done((f32[72,768]{1,0:T(8,128)S(1)}, f32[72,768]{1,0:T(8,128)S(1)}, u32[]{:S(2)}, u32[]{:S(2)}) %collective-permute-start.85) | collective-permute-done | bytes 221216 | tf_op jit(solution)/shard_map/ppermute | solution.py:393
  467.5 3.8 shard_map.322
  475.5 6.7 %collective-permute-done.91 = f32[96,768]{1,0:T(8,128)} collective-permute-done((f32[96,768]{1,0:T(8,128)}, f32[96,768]{1,0:T(8,128)}, u32[]{:S(2)}, u32[]{:S(2)}) %collective-permute-start.91) | collective-permute-done | bytes 294944 | tf_op jit(solution)/shard_map/ppermute | solution.py:389
  482.2 4.9 collective-permute-done.93
  490.2 4.5 shard_map.323
  509.0 3.9 shard_map.324
  (561 shorter events, 249.5 us)
Async XLA Ops:
  3.9 36.2 %collective-permute-start = (f32[1344]{0:T(1024)S(1)}, f32[1344]{0:T(1024)S(1)}, u32[]{:S(2)}, u32[]{:S(2)}) collective-permute-start(f32[1344]{0:T(1024)S(1)} %pad_maximum_fusion.38), channel_id=1, source_target_pairs={{0,3},{1,0},{2,1},{3,2},{4,7},{5,4},{6,5},{7,6},{8,11},{9,8},{10,9... | collective-permute-start | bytes 16136 | tf_op jit(solution)/shard_map/ppermute | solution.py:385
  8.9 31.2 %collective-permute-start.1 = (f32[1344]{0:T(1024)S(1)}, f32[1344]{0:T(1024)S(1)}, u32[]{:S(2)}, u32[]{:S(2)}) collective-permute-start(f32[1344]{0:T(1024)S(1)} %pad_maximum_fusion.38), channel_id=1, source_target_pairs={{0,2},{1,3},{2,0},{3,1},{4,6},{5,7},{6,4},{7,5},{8,10},{9,11},{10,... | collective-permute-start | bytes 16136 | tf_op jit(solution)/shard_map/ppermute | solution.py:385
  8.9 31.2 %collective-permute-start.2 = (f32[1344]{0:T(1024)S(1)}, f32[1344]{0:T(1024)S(1)}, u32[]{:S(2)}, u32[]{:S(2)}) collective-permute-start(f32[1344]{0:T(1024)S(1)} %pad_maximum_fusion.38), channel_id=1, source_target_pairs={{0,1},{1,2},{2,3},{3,0},{4,5},{5,6},{6,7},{7,4},{8,9},{9,10},{10,1... | collective-permute-start | bytes 16136 | tf_op jit(solution)/shard_map/ppermute | solution.py:385
  12.7 27.4 %collective-permute-start.3 = (f32[96,768]{1,0:T(8,128)}, f32[96,768]{1,0:T(8,128)}, u32[]{:S(2)}, u32[]{:S(2)}) collective-permute-start(f32[96,768]{1,0:T(8,128)} %pad_maximum_fusion.25), channel_id=1, source_target_pairs={{0,3},{1,0},{2,1},{3,2},{4,7},{5,4},{6,5},{7,6},{8,11},{9,8},{10,9... | collective-permute-start | bytes 884744 | tf_op jit(solution)/shard_map/ppermute | solution.py:385
  15.5 24.6 %collective-permute-start.4 = (f32[96,768]{1,0:T(8,128)}, f32[96,768]{1,0:T(8,128)}, u32[]{:S(2)}, u32[]{:S(2)}) collective-permute-start(f32[96,768]{1,0:T(8,128)} %pad_maximum_fusion.25), channel_id=1, source_target_pairs={{0,1},{1,2},{2,3},{3,0},{4,5},{5,6},{6,7},{7,4},{8,9},{9,10},{10,1... | collective-permute-start | bytes 884744 | tf_op jit(solution)/shard_map/ppermute | solution.py:385
  100.7 26.3 %collective-permute-start.24 = (f32[192,768]{1,0:T(8,128)}, f32[192,768]{1,0:T(8,128)}, u32[]{:S(2)}, u32[]{:S(2)}) collective-permute-start(f32[192,768]{1,0:T(8,128)} %maximum_convert_fusion.2), channel_id=1, source_target_pairs={{0,2},{1,3},{2,0},{3,1},{4,6},{5,7},{6,4},{7,5},{8,10},{9,11},{10,... | collective-permute-start | bytes 1769480 | tf_op jit(solution)/shard_map/ppermute | solution.py:385
  120.9 23.3 %collective-permute-start.23 = (f32[4,96,768]{2,1,0:T(8,128)S(1)}, f32[4,96,768]{2,1,0:T(8,128)}, u32[]{:S(2)}, u32[]{:S(2)}) collective-permute-start(f32[4,96,768]{2,1,0:T(8,128)S(1)} %constant_dynamic-update-slice_fusion.18.refs_6_), channel_id=1, source_target_pairs={{0,4},{4,0},{8,12},{12,8},{16,20},{20,16},{24,28},{28,24},{1,5},{5... | collective-permute-start | bytes 3538952 | tf_op jit(solution)/shard_map/ppermute | solution.py:393
  230.0 27.4 %collective-permute-start.49 = (f32[2,96,768]{2,1,0:T(8,128)S(1)}, f32[2,96,768]{2,1,0:T(8,128)S(1)}, u32[]{:S(2)}, u32[]{:S(2)}) collective-permute-start(f32[2,96,768]{2,1,0:T(8,128)S(1)} %get-tuple-element.1710), channel_id=1, source_target_pairs={{0,16},{4,20},{8,24},{12,28},{16,0},{20,4},{24,8},{28,12},{1,17},{... | collective-permute-start | bytes 1769480 | tf_op jit(solution)/shard_map/ppermute | solution.py:393
  231.5 25.9 %collective-permute-start.47 = (f32[4,96,768]{2,1,0:T(8,128)}, f32[4,96,768]{2,1,0:T(8,128)S(1)}, u32[]{:S(2)}, u32[]{:S(2)}) collective-permute-start(f32[4,96,768]{2,1,0:T(8,128)} %get-tuple-element.1257), channel_id=1, source_target_pairs={{0,4},{4,0},{8,12},{12,8},{16,20},{20,16},{24,28},{28,24},{1,5},{5... | collective-permute-start | bytes 3538952 | tf_op jit(solution)/shard_map/ppermute | solution.py:393
  231.5 25.9 %collective-permute-start.50 = (f32[4,96,768]{2,1,0:T(8,128)}, f32[4,96,768]{2,1,0:T(8,128)}, u32[]{:S(2)}, u32[]{:S(2)}) collective-permute-start(f32[4,96,768]{2,1,0:T(8,128)} %get-tuple-element.1300), channel_id=1, source_target_pairs={{0,4},{4,0},{8,12},{12,8},{16,20},{20,16},{24,28},{28,24},{1,5},{5... | collective-permute-start | bytes 3538952 | tf_op jit(solution)/shard_map/ppermute | solution.py:393
  258.2 25.7 %collective-permute-start.52 = (f32[4,96,768]{2,1,0:T(8,128)}, f32[4,96,768]{2,1,0:T(8,128)S(1)}, u32[]{:S(2)}, u32[]{:S(2)}) collective-permute-start(f32[4,96,768]{2,1,0:T(8,128)} %get-tuple-element.1324), channel_id=1, source_target_pairs={{0,4},{4,0},{8,12},{12,8},{16,20},{20,16},{24,28},{28,24},{1,5},{5... | collective-permute-start | bytes 3538952 | tf_op jit(solution)/shard_map/ppermute | solution.py:393
  258.4 25.6 %collective-permute-start.55 = (f32[4,96,768]{2,1,0:T(8,128)}, f32[4,96,768]{2,1,0:T(8,128)S(1)}, u32[]{:S(2)}, u32[]{:S(2)}) collective-permute-start(f32[4,96,768]{2,1,0:T(8,128)} %get-tuple-element.1365), channel_id=1, source_target_pairs={{0,4},{4,0},{8,12},{12,8},{16,20},{20,16},{24,28},{28,24},{1,5},{5... | collective-permute-start | bytes 3538952 | tf_op jit(solution)/shard_map/ppermute | solution.py:393
  260.9 22.0 %collective-permute-start.56 = (f32[2,96,768]{2,1,0:T(8,128)}, f32[2,96,768]{2,1,0:T(8,128)}, u32[]{:S(2)}, u32[]{:S(2)}) collective-permute-start(f32[2,96,768]{2,1,0:T(8,128)} %get-tuple-element.1706), channel_id=1, source_target_pairs={{0,16},{4,20},{8,24},{12,28},{16,0},{20,4},{24,8},{28,12},{1,17},{... | collective-permute-start | bytes 1769480 | tf_op jit(solution)/shard_map/ppermute | solution.py:393
  285.0 25.8 %collective-permute-start.62 = (f32[192,768]{1,0:T(8,128)}, f32[192,768]{1,0:T(8,128)}, u32[]{:S(2)}, u32[]{:S(2)}) collective-permute-start(f32[192,768]{1,0:T(8,128)} %pad_maximum_fusion.18), channel_id=1, source_target_pairs={{0,1},{1,2},{2,3},{3,0},{4,5},{5,6},{6,7},{7,4},{8,9},{9,10},{10,1... | collective-permute-start | bytes 1769480 | tf_op jit(solution)/shard_map/ppermute | solution.py:389
  287.5 23.3 %collective-permute-start.59 = (f32[4,96,768]{2,1,0:T(8,128)}, f32[4,96,768]{2,1,0:T(8,128)}, u32[]{:S(2)}, u32[]{:S(2)}) collective-permute-start(f32[4,96,768]{2,1,0:T(8,128)} %get-tuple-element.1394), channel_id=1, source_target_pairs={{0,4},{4,0},{8,12},{12,8},{16,20},{20,16},{24,28},{28,24},{1,5},{5... | collective-permute-start | bytes 3538952 | tf_op jit(solution)/shard_map/ppermute | solution.py:393
  288.5 22.3 %collective-permute-start.60 = (f32[2,96,768]{2,1,0:T(8,128)}, f32[2,96,768]{2,1,0:T(8,128)}, u32[]{:S(2)}, u32[]{:S(2)}) collective-permute-start(f32[2,96,768]{2,1,0:T(8,128)} %get-tuple-element.1702), channel_id=1, source_target_pairs={{0,16},{4,20},{8,24},{12,28},{16,0},{20,4},{24,8},{28,12},{1,17},{... | collective-permute-start | bytes 1769480 | tf_op jit(solution)/shard_map/ppermute | solution.py:393
  313.4 30.9 %collective-permute-start.67 = (f32[192,768]{1,0:T(8,128)}, f32[192,768]{1,0:T(8,128)}, u32[]{:S(2)}, u32[]{:S(2)}) collective-permute-start(f32[192,768]{1,0:T(8,128)} %pad_maximum_fusion.19), channel_id=1, source_target_pairs={{0,3},{1,0},{2,1},{3,2},{4,7},{5,4},{6,5},{7,6},{8,11},{9,8},{10,9... | collective-permute-start | bytes 1769480 | tf_op jit(solution)/shard_map/ppermute | solution.py:389
  319.8 24.5 %collective-permute-start.65 = (f32[4,72,768]{2,1,0:T(8,128)}, f32[4,72,768]{2,1,0:T(8,128)}, u32[]{:S(2)}, u32[]{:S(2)}) collective-permute-start(f32[4,72,768]{2,1,0:T(8,128)} %get-tuple-element.1452), channel_id=1, source_target_pairs={{0,4},{4,0},{8,12},{12,8},{16,20},{20,16},{24,28},{28,24},{1,5},{5... | collective-permute-start | bytes 2654216 | tf_op jit(solution)/shard_map/ppermute | solution.py:393
  322.0 22.3 %collective-permute-start.64 = (f32[2,96,768]{2,1,0:T(8,128)}, f32[2,96,768]{2,1,0:T(8,128)S(1)}, u32[]{:S(2)}, u32[]{:S(2)}) collective-permute-start(f32[2,96,768]{2,1,0:T(8,128)} %get-tuple-element.1700), channel_id=1, source_target_pairs={{0,16},{4,20},{8,24},{12,28},{16,0},{20,4},{24,8},{28,12},{1,17},{... | collective-permute-start | bytes 1769480 | tf_op jit(solution)/shard_map/ppermute | solution.py:393
  345.3 26.6 %collective-permute-start.71 = (f32[192,768]{1,0:T(8,128)}, f32[192,768]{1,0:T(8,128)}, u32[]{:S(2)}, u32[]{:S(2)}) collective-permute-start(f32[192,768]{1,0:T(8,128)} %pad_maximum_fusion.20), channel_id=1, source_target_pairs={{0,2},{1,3},{2,0},{3,1},{4,6},{5,7},{6,4},{7,5},{8,10},{9,11},{10,... | collective-permute-start | bytes 1769480 | tf_op jit(solution)/shard_map/ppermute | solution.py:389
  345.3 26.5 %collective-permute-start.70 = (f32[4,72,768]{2,1,0:T(8,128)}, f32[4,72,768]{2,1,0:T(8,128)}, u32[]{:S(2)}, u32[]{:S(2)}) collective-permute-start(f32[4,72,768]{2,1,0:T(8,128)} %get-tuple-element.1504), channel_id=1, source_target_pairs={{0,4},{4,0},{8,12},{12,8},{16,20},{20,16},{24,28},{28,24},{1,5},{5... | collective-permute-start | bytes 2654216 | tf_op jit(solution)/shard_map/ppermute | solution.py:393
  395.9 32.7 %collective-permute-start.79 = (f32[4,72,768]{2,1,0:T(8,128)}, f32[4,72,768]{2,1,0:T(8,128)}, u32[]{:S(2)}, u32[]{:S(2)}) collective-permute-start(f32[4,72,768]{2,1,0:T(8,128)} %get-tuple-element.1576), channel_id=1, source_target_pairs={{0,4},{4,0},{8,12},{12,8},{16,20},{20,16},{24,28},{28,24},{1,5},{5... | collective-permute-start | bytes 2654216 | tf_op jit(solution)/shard_map/ppermute | solution.py:393
  398.4 30.1 %collective-permute-start.81 = (f32[2,72,768]{2,1,0:T(8,128)}, f32[2,72,768]{2,1,0:T(8,128)}, u32[]{:S(2)}, u32[]{:S(2)}) collective-permute-start(f32[2,72,768]{2,1,0:T(8,128)} %get-tuple-element.1720), channel_id=1, source_target_pairs={{0,16},{4,20},{8,24},{12,28},{16,0},{20,4},{24,8},{28,12},{1,17},{... | collective-permute-start | bytes 1327112 | tf_op jit(solution)/shard_map/ppermute | solution.py:393
  399.7 28.8 %collective-permute-start.78 = (f32[2,96,768]{2,1,0:T(8,128)S(1)}, f32[2,96,768]{2,1,0:T(8,128)}, u32[]{:S(2)}, u32[]{:S(2)}) collective-permute-start(f32[2,96,768]{2,1,0:T(8,128)S(1)} %pad_maximum_fusion.22), channel_id=1, source_target_pairs={{0,8},{4,12},{8,0},{12,4},{16,24},{20,28},{24,16},{28,20},{1,9},{5... | collective-permute-start | bytes 1769480 | tf_op jit(solution)/shard_map/ppermute | solution.py:393
  400.4 28.1 %collective-permute-start.77 = (f32[2,96,768]{2,1,0:T(8,128)S(1)}, f32[2,96,768]{2,1,0:T(8,128)S(1)}, u32[]{:S(2)}, u32[]{:S(2)}) collective-permute-start(f32[2,96,768]{2,1,0:T(8,128)S(1)} %pad_maximum_fusion.21), channel_id=1, source_target_pairs={{0,16},{4,20},{8,24},{12,28},{16,0},{20,4},{24,8},{28,12},{1,17},{... | collective-permute-start | bytes 1769480 | tf_op jit(solution)/shard_map/ppermute | solution.py:393
  405.0 23.6 %collective-permute-start.80 = (f32[72,768]{1,0:T(8,128)}, f32[72,768]{1,0:T(8,128)S(1)}, u32[]{:S(2)}, u32[]{:S(2)}) collective-permute-start(f32[72,768]{1,0:T(8,128)} %get-tuple-element.1764), channel_id=1, source_target_pairs={{0,16},{4,20},{8,24},{12,28},{16,0},{20,4},{24,8},{28,12},{1,17},{... | collective-permute-start | bytes 663560 | tf_op jit(solution)/shard_map/ppermute | solution.py:393
  430.8 22.7 %collective-permute-start.83 = (f32[4,96,768]{2,1,0:T(8,128)S(1)}, f32[4,96,768]{2,1,0:T(8,128)S(1)}, u32[]{:S(2)}, u32[]{:S(2)}) collective-permute-start(f32[4,96,768]{2,1,0:T(8,128)S(1)} %constant_dynamic-update-slice_fusion.34), channel_id=1, source_target_pairs={{0,4},{4,0},{8,12},{12,8},{16,20},{20,16},{24,28},{28,24},{1,5},{5... | collective-permute-start | bytes 3538952 | tf_op jit(solution)/shard_map/ppermute | solution.py:393
  430.9 22.5 %collective-permute-start.82 = (f32[4,96,768]{2,1,0:T(8,128)S(1)}, f32[4,96,768]{2,1,0:T(8,128)S(1)}, u32[]{:S(2)}, u32[]{:S(2)}) collective-permute-start(f32[4,96,768]{2,1,0:T(8,128)S(1)} %constant_dynamic-update-slice_fusion.32), channel_id=1, source_target_pairs={{0,4},{4,0},{8,12},{12,8},{16,20},{20,16},{24,28},{28,24},{1,5},{5... | collective-permute-start | bytes 3538952 | tf_op jit(solution)/shard_map/ppermute | solution.py:393
  431.8 50.4 %collective-permute-start.89 = (f32[512,768]{1,0:T(8,128)S(1)}, f32[512,768]{1,0:T(8,128)S(1)}, u32[]{:S(2)}, u32[]{:S(2)}) collective-permute-start(f32[512,768]{1,0:T(8,128)S(1)} %slice.756), channel_id=1, source_target_pairs={{0,1},{1,0},{2,3},{3,2},{4,5},{5,4},{6,7},{7,6},{8,9},{9,8},{10,11... | collective-permute-start | bytes 4718600 | tf_op jit(solution)/shard_map/ppermute | solution.py:886
  450.8 24.8 %collective-permute-start.92 = (f32[96,768]{1,0:T(8,128)S(1)}, f32[96,768]{1,0:T(8,128)}, u32[]{:S(2)}, u32[]{:S(2)}) collective-permute-start(f32[96,768]{1,0:T(8,128)S(1)} %pad_maximum_fusion.31), channel_id=1, source_target_pairs={{0,2},{1,3},{2,0},{3,1},{4,6},{5,7},{6,4},{7,5},{8,10},{9,11},{10,... | collective-permute-start | bytes 884744 | tf_op jit(solution)/shard_map/ppermute | solution.py:389
  455.0 27.2 %collective-permute-start.91 = (f32[96,768]{1,0:T(8,128)}, f32[96,768]{1,0:T(8,128)}, u32[]{:S(2)}, u32[]{:S(2)}) collective-permute-start(f32[96,768]{1,0:T(8,128)} %pad_maximum_fusion.30), channel_id=1, source_target_pairs={{0,1},{1,2},{2,3},{3,0},{4,5},{5,6},{6,7},{7,4},{8,9},{9,10},{10,1... | collective-permute-start | bytes 884744 | tf_op jit(solution)/shard_map/ppermute | solution.py:389
  459.2 27.8 %collective-permute-start.93 = (f32[96,768]{1,0:T(8,128)}, f32[96,768]{1,0:T(8,128)}, u32[]{:S(2)}, u32[]{:S(2)}) collective-permute-start(f32[96,768]{1,0:T(8,128)} %pad_maximum_fusion.32), channel_id=1, source_target_pairs={{0,3},{1,0},{2,1},{3,2},{4,7},{5,4},{6,5},{7,6},{8,11},{9,8},{10,9... | collective-permute-start | bytes 884744 | tf_op jit(solution)/shard_map/ppermute | solution.py:389
  (149 other events, 1378.8 us)
